TPU v7x, 32 devices: a whole 2x2x4 slice. The times are simulated.
32 devices in a mesh: seq: 16 (over z, x, core), head: 2 (over y).
Axes of the slice: x: 2, y: 2, z: 4, core: 2. Of those that a mesh axis runs over, the one named last changes fastest.
Arguments:
- queries: bfloat16 [4096, 1024], P(('seq', 'head')), may hold values from -10 to 10, as said below
- keys: bfloat16 [4096, 1024], P(('seq', 'head')), may hold values from -8 to 8, as said below
- values: bfloat16 [4096, 1024], P(('seq', 'head')), may hold values from -6 to 6
- grad_out: bfloat16 [4096, 1024], P(('seq', 'head')), may hold values from -6 to 6
- doc_ids: int32 [4096], replicated, may hold values from 0 to 2, never falling along the last dimension, each value on 1 to 2048 neighbouring positions
Outputs:
- attended: bfloat16 [4096, 1024], P(('seq', 'head'))
- grad_queries: bfloat16 [4096, 1024], P(('seq', 'head'))
- grad_keys: bfloat16 [4096, 1024], P(('seq', 'head'))
- grad_values: bfloat16 [4096, 1024], P(('seq', 'head'))
Inputs may be any that keep to these rules, and one draw needn't show every extreme that they name: `queries`: Real-valued entries. `keys`: Real-valued entries. `doc_ids`: document ids never fall along the sequence; the longest document holds exactly half of the 4096 tokens.
All inputs are finite; a program needn't handle non-finite values.
Results may differ from a plain program's by a relative error of at most 0.011.
Values may be sent and summed in bfloat16 or wider, within the bound.
No kernel may reach another device: no remote copies, remote signals or barrier semaphores. Data moves between devices by JAX's collectives and lax.ppermute only.
A program may use at most 128 MiB of HBM per device.

v0:
```python
import dataclasses
import functools

import jax
import jax.numpy as jnp
from jax import lax
from jax.experimental import pallas as pl
from jax.experimental.pallas import tpu as pltpu
from jax.sharding import PartitionSpec as P

HEAD_DIM = 64
LANES = 2 * HEAD_DIM
HIDDEN = -131072.0
DOC_LANE, TOTAL_LANE, QUERY_PAD, KEY_PAD = HEAD_DIM, HEAD_DIM + 3, HEAD_DIM + 6, HEAD_DIM + 7
QUERY_TILE = 256
FAR_ROWS = 8
COPY_PARTS = 2
PACK_LIMIT = 56 * 1024 * 1024
VMEM_LIMIT = 14 * 1024 * 1024


def dot(a, b, contract):
    return lax.dot_general(a, b, ((contract[:1], contract[1:]), ((), ())), preferred_element_type=jnp.float32)


def row_order(rows, rates, shape, axis):
    row = lax.broadcasted_iota(jnp.int32, shape, axis)
    order = row * rates[-1]
    for rate, above in zip(rates[-2::-1], rates[:0:-1]):
        between, fresh = above // rate - 1, row - rows // above
        if between > 0:
            group = fresh if between == 1 else lax.div(fresh, between)
            order = jnp.where(fresh >= 0, group * above + (fresh - group * between + 1) * rate, order)
    return order


def lane_of(shape):
    return lax.broadcasted_iota(jnp.int32, shape, 1)


def halves_swapped(x):
    return jnp.concatenate([x[:, HEAD_DIM:], x[:, :HEAD_DIM]], axis=1)


def lane_mask(rows, at_low, at_high):
    return jnp.where(lane_of((rows, LANES)) < HEAD_DIM, at_low, at_high).astype(jnp.bfloat16)


def pack_kernel(rates, q_hbm, k_hbm, v_hbm, g_hbm, out_hbm, q_ref, k_ref, v_ref, g_ref, out_ref, arrived, left):
    rows, width = q_ref.shape
    copies, outgoing = [], []
    for part in range(COPY_PARTS):
        cols = pl.ds(part * (width // COPY_PARTS), width // COPY_PARTS)
        held = ((q_hbm, q_ref), (k_hbm, k_ref), (v_hbm, v_ref), (g_hbm, g_ref))
        copies.append(
            [pltpu.make_async_copy(a.at[:, cols], b.at[:, cols], arrived.at[part, i]) for i, (a, b) in enumerate(held)]
        )
    for part in copies:
        for copy in part:
            copy.start()
    order = row_order(rows, rates, (rows, rows), 0)
    lane = lane_of((rows, rows))
    low, high = lane_mask(rows, 1.0, 0.0), lane_mask(rows, 0.0, 1.0)
    for tile in range(width // LANES):
        cols = slice(tile * LANES, (tile + 1) * LANES)
        part, inside = divmod(tile * LANES, width // COPY_PARTS)
        if inside == 0:
            for copy in copies[part]:
                copy.wait()
        pairs = ((q_ref[:, cols], g_ref[:, cols]), (k_ref[:, cols], v_ref[:, cols]))
        even = [first * low + halves_swapped(second) * high for first, second in pairs]
        odd = [halves_swapped(first) * low + second * high for first, second in pairs]
        for side, sources in enumerate((even, odd)):
            pick = jnp.where(order == ((lane - (2 * tile + side)) & (rows - 1)), 1.0, 0.0).astype(jnp.bfloat16)
            moved = dot(pick, jnp.concatenate(sources, axis=1), (1, 0)).astype(jnp.bfloat16)
            out_ref[2 * tile + side, 0] = moved[:, :LANES]
            out_ref[2 * tile + side, 1] = moved[:, LANES:]
        if inside + LANES == width // COPY_PARTS:
            done = pl.ds(part * (width // HEAD_DIM // COPY_PARTS), width // HEAD_DIM // COPY_PARTS)
            outgoing.append(pltpu.make_async_copy(out_ref.at[done], out_hbm.at[done], left.at[part]))
            outgoing[-1].start()
    for copy in outgoing:
        copy.wait()


def unpack_kernel(rates, in_ref, *refs):
    (out_hbm, dq_hbm, dk_hbm, dv_hbm), (out_ref, dq_ref, dk_ref, dv_ref, left) = refs[:4], refs[4:]
    rows, width = out_ref.shape
    outgoing = []
    order = row_order(rows, rates, (rows, rows), 1)
    token = lax.broadcasted_iota(jnp.int32, (rows, rows), 0)
    low, high = lane_mask(rows, 1.0, 0.0), lane_mask(rows, 0.0, 1.0)
    for tile in range(width // LANES):
        cols = slice(tile * LANES, (tile + 1) * LANES)
        picks, sources = [], []
        for side in range(2):
            head = 2 * tile + side
            picks.append(jnp.where(((order + head) & (rows - 1)) == token, 1.0, 0.0).astype(jnp.bfloat16))
            columns = []
            for kind in range(2):
                x = in_ref[head, kind]
                y = halves_swapped(x)
                columns += [y * high, x * high] if side else [x * low, y * low]
            sources.append(jnp.concatenate(columns, axis=1))
        moved = dot(jnp.concatenate(picks, axis=1), jnp.concatenate(sources, axis=0), (1, 0)).astype(jnp.bfloat16)
        for i, ref in enumerate((dq_ref, out_ref, dk_ref, dv_ref)):
            ref[:, cols] = moved[:, i * LANES : (i + 1) * LANES]
        part, inside = divmod((tile + 1) * LANES, width // COPY_PARTS)
        if inside == 0:
            done = pl.ds((part - 1) * (width // COPY_PARTS), width // COPY_PARTS)
            held = ((out_ref, out_hbm), (dq_ref, dq_hbm), (dk_ref, dk_hbm), (dv_ref, dv_hbm))
            for i, (a, b) in enumerate(held):
                outgoing.append(pltpu.make_async_copy(a.at[:, done], b.at[:, done], left.at[part - 1, i]))
                outgoing[-1].start()
    for copy in outgoing:
        copy.wait()


@dataclasses.dataclass(frozen=True)
class Plan:
    heads: int
    rows: int
    rates: tuple
    near: tuple
    far: tuple

    @property
    def late(self):
        return self.near[2:], max([count for count, _ in self.near[2:]] + [held for _, held, _ in self.far])


def plan_of(rows, width, shards, parts):
    heads, rates = width // HEAD_DIM, (1, 2, 8, shards)
    near, far = [], []
    for rate in rates:
        span = rows * parts * rate
        if span <= rows * heads:
            near.append((rows // rate, span // rows))
        else:
            far.append((rows // rate, max(rows // rate, FAR_ROWS), span // (rows * heads)))
    return Plan(heads, rows, rates, tuple(near), tuple(far))


def my_place(heads):
    index = lax.axis_index("seq") * lax.axis_size("head") + lax.axis_index("head")
    return lax.div(index, heads), index & (heads - 1)


def rows_of(ref, blocks, count):
    if count == ref.shape[1]:
        return ref[blocks.start : blocks.stop].reshape(len(blocks) * count, LANES)
    if ref.dtype == jnp.bfloat16 and count % 16:
        held = -(-count // 16) * 16
        parts = [ref[j, 0:held].astype(jnp.float32)[0:count] for j in blocks]
        return jnp.concatenate(parts, axis=0).astype(jnp.bfloat16)
    return jnp.concatenate([ref[j, 0:count] for j in blocks], axis=0)


def set_rows(ref, blocks, count, value):
    for i, j in enumerate(blocks):
        ref[j, 0:count] = value[i * count : (i + 1) * count]


def add_rows(ref, blocks, count, value):
    set_rows(ref, blocks, count, rows_of(ref, blocks, count) + value)


def doc_lanes(doc_ref, rows):
    docs = doc_ref[...]
    first, second = [jnp.sum(jnp.where(docs < d, 1, 0)) for d in (1, 2)]
    lane, last = lane_of((rows, LANES)), jnp.iinfo(jnp.int32).max
    start, stop = jnp.full((rows, LANES), last, jnp.int32), jnp.full((rows, LANES), 0, jnp.int32)
    for at, lo, hi in ((0, 0, first), (1, first, second), (2, second, last), (KEY_PAD - DOC_LANE, 0, last)):
        start = jnp.where(lane == DOC_LANE + at, lo, start)
        stop = jnp.where(lane == DOC_LANE + at, hi, stop)
    return start, stop


def key_lanes(marked, lane, padding):
    outside = jnp.where((lane >= TOTAL_LANE) & (lane <= QUERY_PAD), 1.0, 0.0)
    outside = jnp.where((lane >= DOC_LANE) & (lane < TOTAL_LANE), HIDDEN, outside)
    value = jnp.where(marked, 0.0, outside)
    if padding is not None:
        value = jnp.where((lane == KEY_PAD) & padding, HIDDEN, value)
    return value.astype(jnp.bfloat16)


def far_operands(plan, level, doc_ref, qa, ka, va, far_ref):
    count, held, chunks = plan.far[level]
    heads, rows = plan.heads, plan.rows
    chunk, head = my_place(heads)
    every, shape = range(heads), (heads * held, LANES)
    lane, index = lane_of(shape), lax.broadcasted_iota(jnp.int32, shape, 0)
    low, high = lane_mask(shape[0], 1.0, 0.0), lane_mask(shape[0], 0.0, 1.0)
    padding = None if count == held else (index & (held - 1)) >= count
    queries = rows_of(qa, every, held)
    key_sets, value_sets = [rows_of(ka, every, held)], [rows_of(va, every, held)]
    if padding is not None:
        queries = jnp.where((lane == QUERY_PAD) & padding, HIDDEN, queries.astype(jnp.float32)).astype(jnp.bfloat16)
        own = jnp.where((lane == KEY_PAD) & padding, HIDDEN, key_sets[0].astype(jnp.float32))
        key_sets[0] = own.astype(jnp.bfloat16)
    start, stop = doc_lanes(doc_ref, shape[0])
    order = row_order(rows, plan.rates, (held, LANES), 0)
    spots = jnp.concatenate([(order + head) & (rows - 1)] * heads, axis=0)
    for i in range(1, chunks):
        token = ((chunk ^ i) * heads + lax.div(index, held)) * rows + spots
        marked = (token >= start) & (token < stop)
        key_sets.append(far_ref[i - 1] * low + key_lanes(marked, lane, padding))
        value_sets.append(far_ref[i - 1] * high + low)
    return queries, jnp.concatenate(key_sets, axis=0), jnp.concatenate(value_sets, axis=0)


def forward(queries, keys, values):
    scores = dot(queries, keys, (1, 1))
    peak = jnp.max(scores, axis=1, keepdims=True)
    weights = jnp.exp(scores - peak).astype(jnp.bfloat16)
    return jnp.broadcast_to(peak, (queries.shape[0], LANES)), dot(weights, values, (1, 0))


def backward(queries, upstream, keys, values):
    probability = jnp.exp(dot(keys, queries, (1, 1)))
    shifted = (probability * dot(values, upstream, (1, 1))).astype(jnp.bfloat16)
    for_keys = dot(shifted, queries, (1, 0))
    for_values = dot(probability.astype(jnp.bfloat16), upstream, (1, 0))
    key_low = lane_of(for_keys.shape) < HEAD_DIM
    return dot(shifted, keys, (0, 0)), jnp.where(key_low, for_keys, for_values)


def merged(old_peak, old, peak, summed):
    new_peak = jnp.maximum(old_peak, peak)
    return new_peak, old * jnp.exp(old_peak - new_peak) + summed * jnp.exp(peak - new_peak)


def tiles(plan, count, span):
    per_tile = max(1, QUERY_TILE // count)
    for start in range(0, plan.heads, span):
        for begin in range(start, start + span, per_tile):
            yield range(start, start + span), range(begin, min(begin + per_tile, start + span))


def near_kernel(plan, doc_ref, x_ref, qa, ka, va, ga, acc, top):
    heads, rows = plan.heads, plan.rows
    chunk, head = my_place(heads)
    lane = lane_of((rows, LANES))
    spot = (row_order(rows, plan.rates, (rows, LANES), 0) + head) & (rows - 1)
    start, stop = doc_lanes(doc_ref, rows)
    low, high = lane_mask(rows, 1.0, 0.0), lane_mask(rows, 0.0, 1.0)
    low_scaled = lane_mask(rows, HEAD_DIM**-0.5, 0.0)
    for j in range(heads):
        token = (chunk * heads + j) * rows + spot
        marked = (token >= start) & (token < stop)
        qg, kv = x_ref[j, 0], x_ref[j, 1]
        qa[j] = qg * low_scaled + jnp.where(marked, 1.0, 0.0).astype(jnp.bfloat16)
        ka[j] = kv * low + key_lanes(marked, lane, None)
        va[j] = kv * high + low
        ga[j] = qg * high
    for level, (count, span) in enumerate(plan.near):
        for key_blocks, blocks in tiles(plan, count, span):
            peak, summed = forward(*(rows_of(r, b, count) for r, b in ((qa, blocks), (ka, key_blocks), (va, key_blocks))))
            if level > 0:
                peak, summed = merged(rows_of(top, blocks, count), rows_of(acc, blocks, count), peak, summed)
            set_rows(top, blocks, count, peak)
            set_rows(acc, blocks, count, summed)


def pieces(x):
    first = x.astype(jnp.bfloat16).astype(jnp.float32)
    second = (x - first).astype(jnp.bfloat16).astype(jnp.float32)
    return first, second, x - first - second


def in_lanes(x, at):
    first, second, third = pieces(x)
    lane = lane_of(x.shape)
    value = jnp.where(lane == at, first, jnp.where(lane == at + 1, second, jnp.where(lane == at + 2, third, 0.0)))
    return value.astype(jnp.bfloat16)


def far_kernel(plan, doc_ref, qa, ka, va, ga, acc_in, top_in, *refs):
    levels = len(plan.far)
    far_in, refs = refs[:levels], refs[levels:]
    (qb, gb, output), refs = refs[:3], refs[3:]
    far_dq, far_dkv, far_out, (acc, top) = refs[:levels], refs[levels : 2 * levels], refs[2 * levels : -2], refs[-2:]
    heads, rows = plan.heads, plan.rows
    every = range(heads)
    _, reach = plan.late
    for j in every:
        acc[j], top[j] = acc_in[j, 0:reach], top_in[j, 0:reach]
    for level, (_, held, _) in enumerate(plan.far):
        peak, summed = forward(*far_operands(plan, level, doc_ref, qa, ka, va, far_in[level]))
        peak, summed = merged(rows_of(top, every, held), rows_of(acc, every, held), peak, summed)
        set_rows(top, every, held, peak)
        set_rows(acc, every, held, summed)

    low = lane_of((rows, LANES)) < HEAD_DIM
    for j in every:
        summed = jnp.concatenate([acc[j], acc_in[j, reach:]], axis=0)
        peak = jnp.concatenate([top[j], top_in[j, reach:]], axis=0)
        total = jnp.where(low, summed, pltpu.roll(summed, HEAD_DIM, 1))
        normal = summed / total
        upstream = ga[j]
        delta = jnp.sum(normal * upstream.astype(jnp.float32), axis=1, keepdims=True)
        qb[j] = qa[j] + in_lanes(-(peak + jnp.log(total)), TOTAL_LANE)
        gb[j] = upstream + in_lanes(jnp.broadcast_to(-delta, (rows, LANES)), 0)
        output[j] = normal

    for level, (_, held, chunks) in enumerate(plan.far):
        queries, keys, values = far_operands(plan, level, doc_ref, qb, ka, va, far_in[level])
        for_queries, for_keys = backward(queries, rows_of(gb, every, held), keys, values)
        size = heads * held
        far_dq[level][...] = for_queries
        far_dkv[level][...] = for_keys[:size]
        for i in range(1, chunks):
            far_out[level][i - 1] = for_keys[i * size : (i + 1) * size].astype(jnp.bfloat16)


def local_kernel(plan, qb, ka, va, gb, dq, dkv):
    for level, (count, span) in enumerate(plan.near[:2]):
        for key_blocks, blocks in tiles(plan, count, span):
            for_queries, for_keys = backward(
                *(rows_of(r, b, count) for r, b in ((qb, blocks), (gb, blocks), (ka, key_blocks), (va, key_blocks)))
            )
            (add_rows if level else set_rows)(dq, blocks, count, for_queries)
            fresh = level == 0 and blocks.start == key_blocks.start
            (set_rows if fresh else add_rows)(dkv, key_blocks, count, for_keys)


def last_kernel(plan, qb, ka, va, gb, output, dq_in, dkv_in, *refs):
    levels = len(plan.far)
    far_dq, far_dkv, far_back = refs[:levels], refs[levels : 2 * levels], refs[2 * levels : 3 * levels]
    out_ref, dq, dkv = refs[3 * levels :]
    heads, rows = plan.heads, plan.rows
    every, (near, reach) = range(heads), plan.late
    for j in every:
        dq[j], dkv[j] = dq_in[j, 0:reach], dkv_in[j, 0:reach]
    for count, span in near:
        for key_blocks, blocks in tiles(plan, count, span):
            for_queries, for_keys = backward(
                *(rows_of(r, b, count) for r, b in ((qb, blocks), (gb, blocks), (ka, key_blocks), (va, key_blocks)))
            )
            add_rows(dq, blocks, count, for_queries)
            add_rows(dkv, key_blocks, count, for_keys)
    for level, (_, held, chunks) in enumerate(plan.far):
        add_rows(dq, every, held, far_dq[level][...])
        partial = far_dkv[level][...]
        for i in range(1, chunks):
            partial = partial + far_back[level][i - 1].astype(jnp.float32)
        add_rows(dkv, every, held, partial)
    low = lane_of((rows, LANES)) < HEAD_DIM
    for j in every:
        for_queries = jnp.concatenate([dq[j], dq_in[j, reach:]], axis=0)
        out_ref[j, 0] = jnp.where(low, for_queries * HEAD_DIM**-0.5, output[j]).astype(jnp.bfloat16)
        out_ref[j, 1] = jnp.concatenate([dkv[j], dkv_in[j, reach:]], axis=0).astype(jnp.bfloat16)


def landed(x):
    return pltpu.VMEM(x.shape, x.dtype)


def call(kernel, out_shapes, args, scratch=(), flops=0, inputs=pltpu.VMEM, outputs=pltpu.VMEM, limit=VMEM_LIMIT):
    moved = sum(x.size * x.dtype.itemsize for x in (*args, *out_shapes))
    return pl.pallas_call(
        kernel,
        out_shape=out_shapes,
        in_specs=[pl.BlockSpec(memory_space=inputs)] * len(args),
        out_specs=[pl.BlockSpec(memory_space=outputs)] * len(out_shapes),
        scratch_shapes=scratch,
        compiler_params=pltpu.CompilerParams(vmem_limit_bytes=limit),
        cost_estimate=pl.CostEstimate(flops=flops, bytes_accessed=moved, transcendentals=0),
    )(*args)


def body(queries, keys, values, grad_out, doc_ids):
    rows, width = queries.shape
    shards, parts = lax.axis_size("seq"), lax.axis_size("head")
    devices, axes = shards * parts, ("seq", "head")
    plan = plan_of(rows, width, shards, parts)
    heads, _, (_, reach) = plan.heads, plan.far, plan.late
    groups = [[c * heads + h for h in range(heads)] for c in range(devices // heads)]

    def exchange(x):
        return lax.all_to_all(x, axes, 0, 0, axis_index_groups=groups, tiled=True)

    def from_chunk(x, i):
        return lax.ppermute(x, axes, [(d, d ^ (i * heads)) for d in range(devices)])

    def run(kernel, *rest, **more):
        return call(functools.partial(kernel, plan), *rest, **more)

    shape, low, full = jax.ShapeDtypeStruct, jnp.bfloat16, jnp.float32
    packed = shape((heads, 2, rows, LANES), low)
    operand, total = shape((heads, rows, LANES), low), shape((heads, rows, LANES), full)
    prefix = shape((heads, reach, LANES), full)
    own_far = [shape((heads * held, LANES), full) for _, held, _ in plan.far]
    docs = doc_ids.reshape(-1, LANES)

    inputs = (queries, keys, values, grad_out)
    semaphores = pltpu.SemaphoreType.DMA((COPY_PARTS, len(inputs)))
    landing = [landed(x) for x in (*inputs, packed)] + [semaphores, pltpu.SemaphoreType.DMA((COPY_PARTS,))]
    mine = call(
        functools.partial(pack_kernel, plan.rates), [packed], inputs, landing, flops=1 << 27, inputs=pltpu.HBM, outputs=pltpu.HBM, limit=PACK_LIMIT
    )[0]
    chunk = exchange(mine)
    gathered = []
    for _, held, chunks in plan.far:
        picked = chunk[:, 1, :held].reshape(heads * held, LANES)
        gathered.append(jnp.stack([from_chunk(picked, i) for i in range(1, chunks)]))
    qa, ka, va, ga, acc, top = run(near_kernel, [operand] * 4 + [total] * 2, (docs, chunk), flops=1 << 30)
    sent = [shape(x.shape, x.dtype) for x in gathered]
    qb, gb, output, *rest = run(
        far_kernel,
        [operand] * 2 + [total] + own_far * 2 + sent,
        (docs, qa, ka, va, ga, acc, top, *gathered),
        [landed(prefix)] * 2,
        flops=1 << 28,
    )
    owned, partials = rest[: 2 * len(plan.far)], rest[2 * len(plan.far) :]
    returned = [jnp.stack([from_chunk(x[i], i + 1) for i in range(x.shape[0])]) for x in partials]
    dq, dkv = run(local_kernel, [total] * 2, (qb, ka, va, gb), flops=1 << 30)
    grads = run(
        last_kernel, [packed], (qb, ka, va, gb, output, dq, dkv, *owned, *returned), [landed(prefix)] * 2, flops=1 << 28
    )[0]
    result = [shape((rows, width), low)] * 4
    leaving = [landed(x) for x in result] + [semaphores]
    unpack = functools.partial(unpack_kernel, plan.rates)
    return tuple(call(unpack, result, (exchange(grads),), leaving, flops=1 << 27, outputs=pltpu.HBM))


def solution(mesh):
    split = P(("seq", "head"), None)
    return jax.shard_map(
        body, mesh=mesh, in_specs=(split,) * 4 + (P(),), out_specs=(split,) * 4, check_vma=False
    )
```

profile of v0, /device:TPU:0, one launch (start us, length us, event | category | flops | bytes accessed | tf_op | source)
XLA Modules:
  0.0 59.9 jit_solution(14172789008562468402)
XLA Ops:
  0.6 2.8 %shard_map.84 = bf16[16,2,128,128]{3,2,1,0:T(8,128)(2,1)} custom-call(bf16[128,1024]{1,0:T(8,128)(2,1)} %q_hbm.1, bf16[128,1024]{1,0:T(8,128)(2,1)} %k_hbm.1, bf16[128,1024]{1,0:T(8,128)(2,1)} %v_hbm.1, bf16[128,1024]{1,0:T(8,128)(2,1)} %g_hbm.1), custom_call_target="tpu_custom_call" | custom-call | flops 134217728 | bytes 2097152 | tf_op jit(solution)/shard_map/pallas_call | solution.py:362
  3.4 22.1 %all_to_all.10.x_ref = bf16[16,2,128,128]{3,2,1,0:T(8,128)(2,1)S(1)} all-to-all(bf16[16,2,128,128]{3,2,1,0:T(8,128)(2,1)} %shard_map.84), channel_id=1, replica_groups={{0,1,2,3,4,5,6,7,8,9,10,11,12,13,14,15},{16,17,18,19,20,21,22,23,24,25,..., dimensions={0} | all-to-all | bytes 2097152 | tf_op jit(solution)/shard_map/all_to_all | solution.py:382
  25.5 0.0 copy-start
  25.6 2.7 %collective-permute-start = (bf16[128,128]{1,0:T(8,128)(2,1)S(1)}, bf16[128,128]{1,0:T(8,128)(2,1)S(1)}, u32[]{:S(2)}, u32[]{:S(2)}) collective-permute-start(bf16[128,128]{1,0:T(8,128)(2,1)S(1)} %slice_bitcast_fusion), channel_id=1, source_target_pairs={{0,16},{1,17},{2,18},{3,19},{4,20},{5,21},{6,22},{7,23},{8,24},{9,... | collective-permute-start | bytes 98312 | tf_op jit(solution)/shard_map/ppermute | solution.py:385
  28.2 0.0 copy-done
  28.2 1.7 %shard_map.85 = (bf16[16,128,128]{2,1,0:T(8,128)(2,1)S(1)}, bf16[16,128,128]{2,1,0:T(8,128)(2,1)S(1)}, bf16[16,128,128]{2,1,0:T(8,128)(2,1)S(1)}, bf16[16,128,12...) custom-call(s32[32,128]{1,0:T(8,128)S(1)} %bitcast.8, ...), custom_call_target="tpu_custom_call" | custom-call | flops 1073741824 | bytes 5259264 | tf_op jit(solution)/shard_map/pallas_call | solution.py:362
  30.0 0.8 %collective-permute-done = bf16[128,128]{1,0:T(8,128)(2,1)S(1)} collective-permute-done((bf16[128,128]{1,0:T(8,128)(2,1)S(1)}, bf16[128,128]{1,0:T(8,128)(2,1)S(1)}, u32[]{:S(2)}, u32[]{:S(2)}) %collective-permute-start) | collective-permute-done | bytes 32800 | tf_op jit(solution)/shard_map/ppermute | solution.py:385
  30.8 2.0 %shard_map.86 = (bf16[16,128,128]{2,1,0:T(8,128)(2,1)S(1)}, bf16[16,128,128]{2,1,0:T(8,128)(2,1)S(1)}, f32[16,128,128]{2,1,0:T(8,128)S(1)}, f32[128,128]{1,0:T(8...) custom-call(s32[32,128]{1,0:T(8,128)S(1)} %bitcast.9, ...), custom_call_target="tpu_custom_call" | custom-call | flops 268435456 | bytes 6504448 | tf_op jit(solution)/shard_map/pallas_call | solution.py:362
  32.8 2.3 %collective-permute-start.1 = (bf16[128,128]{1,0:T(8,128)(2,1)S(1)}, bf16[128,128]{1,0:T(8,128)(2,1)S(1)}, u32[]{:S(2)}, u32[]{:S(2)}) collective-permute-start(bf16[128,128]{1,0:T(8,128)(2,1)S(1)} %bitcast.10), channel_id=1, source_target_pairs={{0,16},{1,17},{2,18},{3,19},{4,20},{5,21},{6,22},{7,23},{8,24},{9,... | collective-permute-start | bytes 98312 | tf_op jit(solution)/shard_map/ppermute | solution.py:385
  35.1 3.7 %shard_map.87 = (f32[16,128,128]{2,1,0:T(8,128)S(1)}, f32[16,128,128]{2,1,0:T(8,128)S(1)}) custom-call(bf16[16,128,128]{2,1,0:T(8,128)(2,1)S(1)} %get-tuple-element.24.qb, bf16[16,128,128]{2,1,0:T(8,128)(2,1)S(1)} %get-tuple-element.19.ka, bf16[16,128,128]{2,1,0:T(8,128)(2,1)S(1)} %get-tuple-element.20.va, bf16[16,128,128]{2,1,0:T(8,128)(2,1)S(1)} %get-tuple-element.25.gb), custom_call_target="tpu_custom_call" | custom-call | flops 1073741824 | bytes 4194304 | tf_op jit(solution)/shard_map/pallas_call | solution.py:362
  38.8 0.0 collective-permute-done.1
  38.9 0.6 shard_map.88
  39.4 19.1 %all_to_all.11.in_ref = bf16[16,2,128,128]{3,2,1,0:T(8,128)(2,1)S(1)} all-to-all(bf16[16,2,128,128]{3,2,1,0:T(8,128)(2,1)S(1)} %shard_map.88), channel_id=1, replica_groups={{0,1,2,3,4,5,6,7,8,9,10,11,12,13,14,15},{16,17,18,19,20,21,22,23,24,25,..., dimensions={0} | all-to-all | bytes 2097152 | tf_op jit(solution)/shard_map/all_to_all | solution.py:382
  58.5 1.4 %shard_map.89 = (bf16[128,1024]{1,0:T(8,128)(2,1)}, bf16[128,1024]{1,0:T(8,128)(2,1)}, bf16[128,1024]{1,0:T(8,128)(2,1)}, bf16[128,1024]{1,0:T(8,128)(2,1)}) custom-call(bf16[16,2,128,128]{3,2,1,0:T(8,128)(2,1)S(1)} %all_to_all.11.in_ref), custom_call_target="tpu_custom_call" | custom-call | flops 134217728 | bytes 2097152 | tf_op jit(solution)/shard_map/pallas_call | solution.py:362
  (1 shorter events, 0.0 us)
Async XLA Ops:
  25.5 2.7 %copy-start = (s32[4096]{0:T(1024)S(1)}, s32[4096]{0:T(1024)}, u32[]{:S(2)}) copy-start(s32[4096]{0:T(1024)} %param.9) | copy-start | bytes 49156
  25.6 5.2 %collective-permute-start = (bf16[128,128]{1,0:T(8,128)(2,1)S(1)}, bf16[128,128]{1,0:T(8,128)(2,1)S(1)}, u32[]{:S(2)}, u32[]{:S(2)}) collective-permute-start(bf16[128,128]{1,0:T(8,128)(2,1)S(1)} %slice_bitcast_fusion), channel_id=1, source_target_pairs={{0,16},{1,17},{2,18},{3,19},{4,20},{5,21},{6,22},{7,23},{8,24},{9,... | collective-permute-start | bytes 98312 | tf_op jit(solution)/shard_map/ppermute | solution.py:385
  32.8 6.0 %collective-permute-start.1 = (bf16[128,128]{1,0:T(8,128)(2,1)S(1)}, bf16[128,128]{1,0:T(8,128)(2,1)S(1)}, u32[]{:S(2)}, u32[]{:S(2)}) collective-permute-start(bf16[128,128]{1,0:T(8,128)(2,1)S(1)} %bitcast.10), channel_id=1, source_target_pairs={{0,16},{1,17},{2,18},{3,19},{4,20},{5,21},{6,22},{7,23},{8,24},{9,... | collective-permute-start | bytes 98312 | tf_op jit(solution)/shard_map/ppermute | solution.py:385
where the time goes:
time: 60.2 us; the launch traced here: 59.9 us
  blocking collectives  41.2 us (68%)
  Pallas kernels  12.3 us (20%)
  starting transfers between devices  4.96 us (8%)
  waiting for transfers between devices  0.84 us (1%)
  between operations  0.68 us (1%)
    all_to_all x2, blocking collectives, exchange(): return lax.all_to_all(x, axes, 0, 0, axis_index_groups=groups, tiled=True)  41.2 us
    pallas_call x6, Pallas kernels, call(): pl.pallas_call(kernel, out_shape=out_shapes, in_specs=[pl.BlockSpec(memor...  12.3 us
    ppermute x2, starting transfers between devices, from_chunk(): return lax.ppermute(x, axes, [(d, d ^ i * heads) for d in range(devices)])  4.96 us
  transfers between devices with their start and end apart: 2, of which 1 were waited for; matrix products, arithmetic and copies ran while one was open for 0% of the time, Pallas kernels for 9%

commit v1 on v0

v1 whole, which is shorter than its diff:
```python
import dataclasses
import functools

import jax
import jax.numpy as jnp
from jax import lax
from jax.experimental import pallas as pl
from jax.experimental.pallas import tpu as pltpu
from jax.sharding import PartitionSpec as P

HEAD_DIM = 64
LANES = 2 * HEAD_DIM
HIDDEN = -131072.0
DOC_LANE, TOTAL_LANE, QUERY_PAD, KEY_PAD = HEAD_DIM, HEAD_DIM + 3, HEAD_DIM + 6, HEAD_DIM + 7
QUERY_TILE = 256
FAR_ROWS = 8
PACK_LIMIT = 56 * 1024 * 1024
VMEM_LIMIT = 14 * 1024 * 1024


def dot(a, b, contract):
    return lax.dot_general(a, b, ((contract[:1], contract[1:]), ((), ())), preferred_element_type=jnp.float32)


def row_order(rows, rates, shape, axis):
    row = lax.broadcasted_iota(jnp.int32, shape, axis)
    order = row * rates[-1]
    for rate, above in zip(rates[-2::-1], rates[:0:-1]):
        between, fresh = above // rate - 1, row - rows // above
        if between > 0:
            group = fresh if between == 1 else lax.div(fresh, between)
            order = jnp.where(fresh >= 0, group * above + (fresh - group * between + 1) * rate, order)
    return order


def lane_of(shape):
    return lax.broadcasted_iota(jnp.int32, shape, 1)


def halves_swapped(x):
    return jnp.concatenate([x[:, HEAD_DIM:], x[:, :HEAD_DIM]], axis=1)


def lane_mask(rows, at_low, at_high):
    return jnp.where(lane_of((rows, LANES)) < HEAD_DIM, at_low, at_high).astype(jnp.float32).astype(jnp.bfloat16)


@dataclasses.dataclass(frozen=True)
class Plan:
    heads: int
    rows: int
    rates: tuple
    near: tuple
    far: tuple

    bit: int

    @property
    def reach(self):
        return max([16] + [held for _, held, _ in self.far] + [count for count, _ in self.near[2:]])

    @property
    def group(self):
        return max(2 * self.bit, self.near[1][1])

    def group_order(self, base):
        return [m for m in self.order if base <= m < base + self.group]

    @property
    def others(self):
        return max([chunks for _, _, chunks in self.far], default=1) - 1

    @property
    def message(self):
        return 2 * self.rows + self.others * self.reach

    @property
    def steps(self):
        return [m for m in range(self.heads) if not m & self.bit]

    @property
    def order(self):
        every = self.steps[-1]
        pairs = [(every ^ m, m) for m in self.steps[1:-1] if m < every ^ m]
        return [every, *(m for pair in pairs for m in pair), 0]

    def far_place(self, i):
        return 2 * self.rows + (i - 1) * self.reach


def plan_of(rows, width, shards, parts):
    heads, rates = width // HEAD_DIM, (1, 2, 8, shards)
    near, far = [], []
    for rate in rates:
        span = rows * parts * rate
        if span <= rows * heads:
            near.append((rows // rate, span // rows))
        else:
            far.append((rows // rate, max(rows // rate, FAR_ROWS), span // (rows * heads)))
    return Plan(heads, rows, rates, tuple(near), tuple(far), parts)


def my_place(heads):
    index = lax.axis_index("seq") * lax.axis_size("head") + lax.axis_index("head")
    return lax.div(index, heads), index & (heads - 1)


def pack_pair(plan, step, columns, blocks, far):
    rows = plan.rows
    _, me = my_place(plan.heads)
    order = row_order(rows, plan.rates, (rows, rows), 0)
    lane = lane_of((rows, rows))
    low, high = lane_mask(rows, 1.0, 0.0), lane_mask(rows, 0.0, 1.0)
    q, k, v, g = columns
    for side in range(2):
        if side:
            sources = [halves_swapped(first) * low + second * high for first, second in ((q, g), (k, v))]
        else:
            sources = [first * low + halves_swapped(second) * high for first, second in ((q, g), (k, v))]
        head = (me ^ step) & ~1 | side
        pick = jnp.where(order == ((lane - head) & (rows - 1)), 1.0, 0.0).astype(jnp.bfloat16)
        moved = dot(pick, jnp.concatenate(sources, axis=1), (1, 0)).astype(jnp.bfloat16)
        slot = plan.steps.index(step & ~plan.bit) + ((me & 1) ^ side)
        blocks[slot, 0:rows] = moved[:, :LANES]
        blocks[slot, rows : 2 * rows] = moved[:, LANES:]
        far[slot] = moved[: plan.reach, LANES:]


def tile_of(plan, step):
    _, me = my_place(plan.heads)
    return pl.ds(pl.multiple_of(((me ^ step) >> 1) * LANES, LANES), LANES)


def send_kernel(plan, *refs):
    inputs, (blocks, far, held, arrived) = refs[:4], refs[4:]
    steps = [step | plan.bit for step in plan.steps[::2]]
    copies = []
    for n, step in enumerate(steps):
        cols = tile_of(plan, step)
        copies.append(
            [pltpu.make_async_copy(x.at[:, cols], held.at[n, i], arrived.at[n, i]) for i, x in enumerate(inputs)]
        )
        for copy in copies[-1]:
            copy.start()
    for n, step in enumerate(steps):
        for copy in copies[n]:
            copy.wait()
        pack_pair(plan, step, [held[n, i] for i in range(4)], blocks, far)


def keep_kernel(plan, *refs):
    inputs, (blocks, far) = refs[:4], refs[4:]
    for step in plan.steps[::2]:
        cols = tile_of(plan, step)
        pack_pair(plan, step, [x[:, cols] for x in inputs], blocks, far)


def join_kernel(plan, keep, received, *refs):
    same, cross, messages = refs[: plan.others], refs[plan.others : 2 * plan.others], refs[2 * plan.others :]
    for step, message in zip(plan.order, messages):
        slot = plan.steps.index(step)
        for half, (block, far) in enumerate(((keep, same), (received, cross))):
            message[half, 0 : 2 * plan.rows] = block[slot]
            for i in range(1, plan.others + 1):
                at = plan.far_place(i)
                message[half, at : at + plan.reach] = far[i - 1][slot]


def part_kernel(plan, *refs):
    steps = len(plan.steps)
    messages, send, refs = refs[:steps], refs[steps], refs[steps + 1 :]
    same, cross = refs[: plan.others], refs[plan.others :]
    for step, message in zip(plan.order, messages):
        slot = plan.steps.index(step)
        send[slot] = message[1, 0 : 2 * plan.rows]
        for i in range(1, plan.others + 1):
            at = plan.far_place(i)
            same[i - 1][slot] = message[0, at : at + plan.reach]
            cross[i - 1][slot] = message[1, at : at + plan.reach]


def unpack_kernel(plan, *refs):
    steps, others = len(plan.steps), plan.others
    messages, received, refs = refs[:steps], refs[steps], refs[steps + 1 :]
    same, cross, (out_ref, dq_ref, dk_ref, dv_ref) = refs[:others], refs[others : 2 * others], refs[2 * others :]
    rows, width = out_ref.shape
    _, me = my_place(plan.heads)
    order = row_order(rows, plan.rates, (rows, rows), 1)
    token = lax.broadcasted_iota(jnp.int32, (rows, rows), 0)
    masks = []
    for distance in range(2):
        side = (me & 1) ^ distance
        masks.append((lane_mask(rows, 1 - side, 0), lane_mask(rows, 0, side)))
    for step in range(0, plan.heads, 2):
        tile = (me ^ step) >> 1
        cols = pl.ds(pl.multiple_of(tile * LANES, LANES), LANES)
        picks, sources = [], []
        for distance in range(2):
            slot = plan.steps.index(step & ~plan.bit) + distance
            block, far = (received.at[slot], cross) if step & plan.bit else (messages[plan.order.index(plan.steps[slot])].at[0], same)
            x, kv = block[0:rows], block[rows : 2 * rows]
            first = kv[: plan.reach].astype(jnp.float32)
            for ref in far:
                first = first + ref[slot].astype(jnp.float32)
            kv = jnp.concatenate([first.astype(jnp.bfloat16), kv[plan.reach :]], axis=0)
            at_low, at_high = masks[distance]
            columns = []
            for y in (x, kv):
                turned = halves_swapped(y)
                columns += [y * at_low + turned * at_high, turned * at_low + y * at_high]
            picks.append(jnp.where(((order + (me ^ (step + distance))) & (rows - 1)) == token, 1.0, 0.0).astype(jnp.bfloat16))
            sources.append(jnp.concatenate(columns, axis=1))
        moved = dot(jnp.concatenate(picks, axis=1), jnp.concatenate(sources, axis=0), (1, 0)).astype(jnp.bfloat16)
        for i, ref in enumerate((dq_ref, out_ref, dk_ref, dv_ref)):
            ref[:, cols] = moved[:, i * LANES : (i + 1) * LANES]


def rows_of(ref, blocks, count):
    if count == ref.shape[1] and count % 16 == 0:
        return ref[blocks.start : blocks.stop].reshape(len(blocks) * count, LANES)
    if ref.dtype == jnp.bfloat16 and count % 16:
        held = -(-count // 16) * 16
        parts = [ref[j, 0:held].astype(jnp.float32)[0:count] for j in blocks]
        return jnp.concatenate(parts, axis=0).astype(jnp.bfloat16)
    return jnp.concatenate([ref[j, 0:count] for j in blocks], axis=0)


def rows_among(refs, every, count):
    size = refs[0].shape[0]
    return jnp.concatenate([rows_of(refs[j // size], range(j % size, j % size + 1), count) for j in every], axis=0)


def set_rows(ref, blocks, count, value):
    for i, j in enumerate(blocks):
        ref[j, 0:count] = value[i * count : (i + 1) * count]


def add_rows(ref, blocks, count, value):
    set_rows(ref, blocks, count, rows_of(ref, blocks, count) + value)


def doc_lanes(doc_ref, rows):
    docs = doc_ref[...]
    first, second = [jnp.sum(jnp.where(docs < d, 1, 0)) for d in (1, 2)]
    lane, last = lane_of((rows, LANES)), jnp.iinfo(jnp.int32).max
    start, stop = jnp.full((rows, LANES), last, jnp.int32), jnp.full((rows, LANES), 0, jnp.int32)
    for at, lo, hi in ((0, 0, first), (1, first, second), (2, second, last), (KEY_PAD - DOC_LANE, 0, last)):
        start = jnp.where(lane == DOC_LANE + at, lo, start)
        stop = jnp.where(lane == DOC_LANE + at, hi, stop)
    return start, stop


def key_lanes(marked, lane, padding):
    outside = jnp.where((lane >= TOTAL_LANE) & (lane <= QUERY_PAD), 1.0, 0.0)
    outside = jnp.where((lane >= DOC_LANE) & (lane < TOTAL_LANE), HIDDEN, outside)
    value = jnp.where(marked, 0.0, outside)
    if padding is not None:
        value = jnp.where((lane == KEY_PAD) & padding, HIDDEN, value)
    return value.astype(jnp.bfloat16)


def far_operands(plan, level, doc_ref, qa, ka, va, block_of):
    count, held, chunks = plan.far[level]
    heads, rows = plan.heads, plan.rows
    chunk, head = my_place(heads)
    every, shape = range(heads), (heads * held, LANES)
    lane, index = lane_of(shape), lax.broadcasted_iota(jnp.int32, shape, 0)
    low, high = lane_mask(shape[0], 1.0, 0.0), lane_mask(shape[0], 0.0, 1.0)
    padding = None if count == held else (index & (held - 1)) >= count
    queries = rows_among(qa, every, held)
    key_sets, value_sets = [rows_among(ka, every, held)], [rows_among(va, every, held)]
    if padding is not None:
        queries = jnp.where((lane == QUERY_PAD) & padding, HIDDEN, queries.astype(jnp.float32)).astype(jnp.bfloat16)
        own = jnp.where((lane == KEY_PAD) & padding, HIDDEN, key_sets[0].astype(jnp.float32))
        key_sets[0] = own.astype(jnp.bfloat16)
    start, stop = doc_lanes(doc_ref, shape[0])
    order = row_order(rows, plan.rates, (held, LANES), 0)
    spots = jnp.concatenate([(order + head) & (rows - 1)] * heads, axis=0)
    for i in range(1, chunks):
        token = ((chunk ^ i) * heads + (head ^ lax.div(index, held))) * rows + spots
        at = plan.far_place(i)
        parts = [block_of(j)[at : at + plan.reach] for j in every]
        if held < plan.reach:
            parts = [x.astype(jnp.float32)[:held] for x in parts]
        kv = jnp.concatenate(parts, axis=0).astype(jnp.bfloat16)
        marked = (token >= start) & (token < stop)
        key_sets.append(kv * low + key_lanes(marked, lane, padding))
        value_sets.append(kv * high + low)
    return queries, jnp.concatenate(key_sets, axis=0), jnp.concatenate(value_sets, axis=0)


def forward(queries, keys, values):
    scores = dot(queries, keys, (1, 1))
    peak = jnp.max(scores, axis=1, keepdims=True)
    weights = jnp.exp(scores - peak).astype(jnp.bfloat16)
    return jnp.broadcast_to(peak, (queries.shape[0], LANES)), dot(weights, values, (1, 0))


def backward(queries, upstream, keys, values):
    probability = jnp.exp(dot(keys, queries, (1, 1)))
    shifted = (probability * dot(values, upstream, (1, 1))).astype(jnp.bfloat16)
    for_keys = dot(shifted, queries, (1, 0))
    for_values = dot(probability.astype(jnp.bfloat16), upstream, (1, 0))
    key_low = lane_of(for_keys.shape) < HEAD_DIM
    return dot(shifted, keys, (0, 0)), jnp.where(key_low, for_keys, for_values)


def merged(old_peak, old, peak, summed):
    new_peak = jnp.maximum(old_peak, peak)
    return new_peak, old * jnp.exp(old_peak - new_peak) + summed * jnp.exp(peak - new_peak)


def tiles(total, count, span):
    per_tile = max(1, QUERY_TILE // count)
    for start in range(0, total, span):
        for begin in range(start, start + span, per_tile):
            yield range(start, start + span), range(begin, min(begin + per_tile, start + span))


def pieces(x):
    first = x.astype(jnp.bfloat16).astype(jnp.float32)
    second = (x - first).astype(jnp.bfloat16).astype(jnp.float32)
    return first, second, x - first - second


def in_lanes(x, at):
    first, second, third = pieces(x)
    lane = lane_of(x.shape)
    value = jnp.where(lane == at, first, jnp.where(lane == at + 1, second, jnp.where(lane == at + 2, third, 0.0)))
    return value.astype(jnp.bfloat16)


def message_block(plan, refs, order, j):
    return refs[order.index(j & ~plan.bit)].at[1 if j & plan.bit else 0]


def ahead_kernel(plan, base, doc_ref, *refs):
    order = plan.group_order(base)
    x_refs, (qa, ka, va, ga, acc, top) = refs[: len(order)], refs[len(order) :]
    heads, rows = plan.heads, plan.rows
    chunk, head = my_place(heads)
    lane = lane_of((rows, LANES))
    spot = (row_order(rows, plan.rates, (rows, LANES), 0) + head) & (rows - 1)
    start, stop = doc_lanes(doc_ref, rows)
    low, high = lane_mask(rows, 1.0, 0.0), lane_mask(rows, 0.0, 1.0)
    low_scaled = lane_mask(rows, HEAD_DIM**-0.5, 0.0)
    for j in range(plan.group):
        token = (chunk * heads + (head ^ (base + j))) * rows + spot
        marked = (token >= start) & (token < stop)
        x = message_block(plan, x_refs, order, base + j)
        qg, kv = x[0:rows], x[rows : 2 * rows]
        qa[j] = qg * low_scaled + jnp.where(marked, 1.0, 0.0).astype(jnp.bfloat16)
        ka[j] = kv * low + key_lanes(marked, lane, None)
        va[j] = kv * high + low
        ga[j] = qg * high
    for level, (count, span) in enumerate(plan.near[:2]):
        for key_blocks, blocks in tiles(plan.group, count, span):
            peak, summed = forward(*(rows_of(r, b, count) for r, b in ((qa, blocks), (ka, key_blocks), (va, key_blocks))))
            if level > 0:
                peak, summed = merged(rows_of(top, blocks, count), rows_of(acc, blocks, count), peak, summed)
            set_rows(top, blocks, count, peak)
            set_rows(acc, blocks, count, summed)


def middle_kernel(plan, doc_ref, *refs):
    groups, refs = plan.heads // plan.group, list(refs)

    def take(count):
        taken = refs[:count]
        del refs[:count]
        return taken

    x_refs = take(len(plan.steps))
    qa, ka, va, ga, acc_in, top_in, qb, gb, output, dq_out, dkv_out, far_out = [take(groups) for _ in range(12)]
    acc, top, dq, dkv, far_sum = refs
    heads, rows, reach, size = plan.heads, plan.rows, plan.reach, plan.group
    every = range(heads)

    def block_of(j):
        return message_block(plan, x_refs, plan.order, j)

    def near_rows(kinds, key_blocks, blocks, count):
        return [rows_among(refs, key_blocks if is_key else blocks, count) for refs, is_key in kinds]

    for j in every:
        acc[j], top[j] = acc_in[j // size][j % size, 0:reach], top_in[j // size][j % size, 0:reach]

    def join(blocks, count, peak, summed):
        peak, summed = merged(rows_of(top, blocks, count), rows_of(acc, blocks, count), peak, summed)
        set_rows(top, blocks, count, peak)
        set_rows(acc, blocks, count, summed)

    for count, span in plan.near[2:]:
        for key_blocks, blocks in tiles(heads, count, span):
            join(blocks, count, *forward(*near_rows(((qa, 0), (ka, 1), (va, 1)), key_blocks, blocks, count)))
    for level, (_, held, _) in enumerate(plan.far):
        join(every, held, *forward(*far_operands(plan, level, doc_ref, qa, ka, va, block_of)))

    is_low = lane_of((rows, LANES)) < HEAD_DIM
    for j in every:
        g, b = divmod(j, size)
        summed = jnp.concatenate([acc[j], acc_in[g][b, reach:]], axis=0)
        peak = jnp.concatenate([top[j], top_in[g][b, reach:]], axis=0)
        total = jnp.where(is_low, summed, pltpu.roll(summed, HEAD_DIM, 1))
        normal = summed / total
        upstream = ga[g][b]
        delta = jnp.sum(normal * upstream.astype(jnp.float32), axis=1, keepdims=True)
        qb[g][b] = qa[g][b] + in_lanes(-(peak + jnp.log(total)), TOTAL_LANE)
        gb[g][b] = upstream + in_lanes(jnp.broadcast_to(-delta, (rows, LANES)), 0)
        output[g][b] = normal

    dq[...], dkv[...], far_sum[...] = jnp.zeros_like(dq), jnp.zeros_like(dkv), jnp.zeros_like(far_sum)
    for count, span in plan.near[2:]:
        for key_blocks, blocks in tiles(heads, count, span):
            for_queries, for_keys = backward(
                *near_rows(((qb, 0), (gb, 0), (ka, 1), (va, 1)), key_blocks, blocks, count)
            )
            add_rows(dq, blocks, count, for_queries)
            add_rows(dkv, key_blocks, count, for_keys)
    for level, (_, held, chunks) in enumerate(plan.far):
        queries, keys, values = far_operands(plan, level, doc_ref, qb, ka, va, block_of)
        for_queries, for_keys = backward(queries, rows_among(gb, every, held), keys, values)
        whole = heads * held
        add_rows(dq, every, held, for_queries)
        add_rows(dkv, every, held, for_keys[:whole])
        for i in range(1, chunks):
            add_rows(far_sum.at[i - 1], every, held, for_keys[i * whole : (i + 1) * whole])
    for j in every:
        g, b = divmod(j, size)
        dq_out[g][b], dkv_out[g][b] = dq[j], dkv[j]
        for i in range(plan.others):
            far_out[g][b, i * reach : (i + 1) * reach] = far_sum[i, j].astype(jnp.bfloat16)


def behind_kernel(plan, base, qb, ka, va, gb, output, dq_in, dkv_in, far_in, *refs):
    out_refs, (dq, dkv) = refs[:-2], refs[-2:]
    rows, every = plan.rows, range(plan.group)
    for level, (count, span) in enumerate(plan.near[:2]):
        for key_blocks, blocks in tiles(plan.group, count, span):
            for_queries, for_keys = backward(
                *(rows_of(r, b, count) for r, b in ((qb, blocks), (gb, blocks), (ka, key_blocks), (va, key_blocks)))
            )
            (add_rows if level else set_rows)(dq, blocks, count, for_queries)
            fresh = level == 0 and blocks.start == key_blocks.start
            (set_rows if fresh else add_rows)(dkv, key_blocks, count, for_keys)
    add_rows(dq, every, plan.reach, rows_of(dq_in, every, plan.reach))
    add_rows(dkv, every, plan.reach, rows_of(dkv_in, every, plan.reach))
    is_low = lane_of((rows, LANES)) < HEAD_DIM
    for j in every:
        out = message_block(plan, out_refs, plan.group_order(base), base + j)
        out[0:rows] = jnp.where(is_low, dq[j] * HEAD_DIM**-0.5, output[j]).astype(jnp.bfloat16)
        out[rows : 2 * rows] = dkv[j].astype(jnp.bfloat16)
        if plan.others:
            out[2 * rows :] = far_in[j]


def landed(x):
    return pltpu.VMEM(x.shape, x.dtype)


def call(kernel, out_shapes, args, scratch=(), flops=0, inputs=pltpu.VMEM, limit=VMEM_LIMIT):
    moved = sum(x.size * x.dtype.itemsize for x in (*args, *out_shapes))
    return pl.pallas_call(
        kernel,
        out_shape=out_shapes,
        in_specs=[pl.BlockSpec(memory_space=inputs)] * len(args),
        out_specs=[pl.BlockSpec(memory_space=pltpu.VMEM)] * len(out_shapes),
        scratch_shapes=scratch,
        compiler_params=pltpu.CompilerParams(vmem_limit_bytes=limit),
        cost_estimate=pl.CostEstimate(flops=flops, bytes_accessed=moved, transcendentals=0),
    )(*args)


def body(queries, keys, values, grad_out, doc_ids):
    rows, width = queries.shape
    shards, parts = lax.axis_size("seq"), lax.axis_size("head")
    devices = shards * parts
    plan = plan_of(rows, width, shards, parts)
    heads, steps, others = plan.heads, plan.steps, range(1, plan.others + 1)

    def swap(x, distance):
        return lax.ppermute(x, ("seq", "head"), [(d, d ^ distance) for d in range(devices)])

    def run(kernel, *rest, **more):
        return call(functools.partial(kernel, plan), *rest, **more)

    def array(*dims, dtype=jnp.bfloat16):
        return jax.ShapeDtypeStruct((*dims, LANES), dtype)

    blocks, far = array(len(steps), 2 * rows), array(len(steps), plan.reach)
    inputs = (queries, keys, values, grad_out)
    landing = [landed(array(len(steps) // 2, 4, rows)), pltpu.SemaphoreType.DMA((len(steps) // 2, 4))]

    def first_stage(send, same, cross):
        moved = [swap(cross[i - 1], i * heads ^ plan.bit) for i in others]
        moved = [swap(same[i - 1], i * heads) for i in others] + moved
        return [swap(send, plan.bit), *moved]

    send, cross = run(
        send_kernel, [blocks, far], inputs, landing, flops=1 << 26, inputs=pltpu.HBM, limit=PACK_LIMIT
    )
    keep, same = run(keep_kernel, [blocks, far], inputs, flops=1 << 26)
    arrived = first_stage(send, [same] * plan.others, [cross] * plan.others)
    message = array(2, plan.message)
    joined = run(join_kernel, [message] * len(steps), (keep, *arrived))
    chunk = [swap(x, step) if step else x for x, step in zip(joined, plan.order)]

    docs, bases, size, full = doc_ids.reshape(-1, LANES), range(0, heads, plan.group), plan.group, jnp.float32
    operand, total, prefix = array(size, rows), array(size, rows, dtype=full), array(size, plan.reach, dtype=full)
    ahead = [
        call(
            functools.partial(ahead_kernel, plan, base),
            [operand] * 4 + [total] * 2,
            (docs, *(chunk[plan.order.index(m)] for m in plan.group_order(base))),
            flops=1 << 28,
        )
        for base in bases
    ]
    qa, ka, va, ga, acc, top = zip(*ahead)
    scratch = [array(heads, plan.reach, dtype=full)] * 4 + [array(max(1, plan.others), heads, plan.reach, dtype=full)]
    far_part = array(size, max(1, plan.others) * plan.reach)
    middle = run(
        middle_kernel,
        [x for x in (operand, operand, total, prefix, prefix, far_part) for _ in bases],
        (docs, *chunk, *qa, *ka, *va, *ga, *acc, *top),
        [landed(x) for x in scratch],
        flops=1 << 28,
    )
    state = [middle[n :: len(bases)] for n in range(len(bases))]
    grads = {}
    for base, ka_part, va_part, (qb, gb, *others_in) in zip(bases, ka, va, state):
        names = plan.group_order(base)
        parts_out = call(
            functools.partial(behind_kernel, plan, base),
            [message] * len(names),
            (qb, ka_part, va_part, gb, *others_in),
            [landed(total)] * 2,
            flops=1 << 28,
        )
        grads.update(zip(names, parts_out))
    back = [swap(grads[step], step) if step else grads[step] for step in plan.order]
    sent = run(part_kernel, [blocks] + [far] * (2 * plan.others), back)
    returned = first_stage(sent[0], sent[1 : 1 + plan.others], sent[1 + plan.others :])
    result = [jax.ShapeDtypeStruct((rows, width), jnp.bfloat16)] * 4
    return tuple(run(unpack_kernel, result, (*back, *returned), flops=1 << 27))


def solution(mesh):
    split = P(("seq", "head"), None)
    return jax.shard_map(
        body, mesh=mesh, in_specs=(split,) * 4 + (P(),), out_specs=(split,) * 4, check_vma=False
    )
```

time: 60.2 us -> 62.6 us (1.040)
  blocking collectives: 41.2 us -> 0 us
  starting transfers between devices: 4.96 us -> 29 us
  waiting for transfers between devices: 0.84 us -> 17.2 us
  Pallas kernels: 12.3 us -> 15.5 us
    all_to_all x2 -> x0, blocking collectives: 41.2 us -> none  [exchange(): return lax.all_to_all(x, axes, 0, 0, axis_index_groups=groups, tiled=True)]
    ppermute x2 -> x20, starting transfers between devices: 4.96 us -> 29 us  [swap(): lax.ppermute(x, ('seq', 'head'), [(d, d ^ distance) for d in range(device...]
    ppermute x2 -> x20, waiting for transfers between devices: 0.84 us -> 17.2 us  [swap(): lax.ppermute(x, ('seq', 'head'), [(d, d ^ distance) for d in range(device...]
    pallas_call x6 -> x14, Pallas kernels: 12.3 us -> 15.5 us  [call(): pl.pallas_call(kernel, out_shape=out_shapes, in_specs=[pl.BlockSpec(memor...]
  transfers between devices with their start and end apart: 2 -> 20, of which waited for: 1 -> 10; matrix products, arithmetic and copies ran while one was open for 0% -> 0% of each run, Pallas kernels for 9% -> 10%
where the time goes in v1:
time: 62.6 us; the launch traced here: 62.4 us
  starting transfers between devices  29 us (46%)
  waiting for transfers between devices  17.2 us (27%)
  Pallas kernels  15.5 us (25%)
  between operations  0.8 us (1%)
    ppermute x20, starting transfers between devices, swap(): lax.ppermute(x, ('seq', 'head'), [(d, d ^ distance) for d in range(device...  29 us
    ppermute x20, waiting for transfers between devices, swap(): lax.ppermute(x, ('seq', 'head'), [(d, d ^ distance) for d in range(device...  17.2 us
    pallas_call x14, Pallas kernels, call(): pl.pallas_call(kernel, out_shape=out_shapes, in_specs=[pl.BlockSpec(memor...  15.5 us
  transfers between devices with their start and end apart: 20, of which 10 were waited for; matrix products, arithmetic and copies ran while one was open for 0% of the time, Pallas kernels for 10%

profile of v1, /device:TPU:0, one launch (start us, length us, event | category | flops | bytes accessed | tf_op | source)
XLA Modules:
  0.0 62.4 jit_solution(17239019807287433184)
XLA Ops:
  0.6 0.0 copy-start.3
  0.6 0.0 copy-start.2
  0.7 0.0 copy-start.1
  0.7 0.0 copy-start
  0.7 2.9 %shard_map.85 = (bf16[8,256,128]{2,1,0:T(8,128)(2,1)}, bf16[8,16,128]{2,1,0:T(8,128)(2,1)}) custom-call(bf16[128,1024]{1,0:T(8,128)(2,1)} %refs_0_.3, bf16[128,1024]{1,0:T(8,128)(2,1)} %refs_1_.3, bf16[128,1024]{1,0:T(8,128)(2,1)} %refs_2_.3, bf16[128,1024]{1,0:T(8,128)(2,1)} %refs_3_.3), custom_call_target="tpu_custom_call" | custom-call | flops 67108864 | bytes 1605632 | tf_op jit(solution)/shard_map/pallas_call | solution.py:463
  3.6 0.5 collective-permute-start
  4.1 3.7 %collective-permute-start.2 = (bf16[8,16,128]{2,1,0:T(8,128)(2,1)}, bf16[8,16,128]{2,1,0:T(8,128)(2,1)S(1)}, u32[]{:S(2)}, u32[]{:S(2)}) collective-permute-start(bf16[8,16,128]{2,1,0:T(8,128)(2,1)} %get-tuple-element.78), channel_id=1, source_target_pairs={{0,18},{1,19},{2,16},{3,17},{4,22},{5,23},{6,20},{7,21},{8,26},{9,... | collective-permute-start | bytes 98312 | tf_op jit(solution)/shard_map/ppermute | solution.py:482
  7.8 0.0 copy-done.3
  7.8 0.0 copy-done.2
  7.8 0.0 copy-done.1
  7.8 0.0 copy-done
  7.8 0.4 shard_map.84
  8.3 0.1 collective-permute-start.1
  8.3 1.4 %collective-permute-done.2.refs_1_ = bf16[8,16,128]{2,1,0:T(8,128)(2,1)S(1)} collective-permute-done((bf16[8,16,128]{2,1,0:T(8,128)(2,1)}, bf16[8,16,128]{2,1,0:T(8,128)(2,1)S(1)}, u32[]{:S(2)}, u32[]{:S(2)}) %collective-permute-start.2) | collective-permute-done | bytes 32800 | tf_op jit(solution)/shard_map/ppermute | solution.py:482
  9.7 3.8 %collective-permute-done.1.refs_0_ = bf16[8,16,128]{2,1,0:T(8,128)(2,1)S(1)} collective-permute-done((bf16[8,16,128]{2,1,0:T(8,128)(2,1)S(1)}, bf16[8,16,128]{2,1,0:T(8,128)(2,1)S(1)}, u32[]{:S(2)}, u32[]{:S(2)}) %collective-permute-start.1) | collective-permute-done | bytes 32800 | tf_op jit(solution)/shard_map/ppermute | solution.py:482
  13.5 0.0 collective-permute-done.received
  13.5 0.0 copy-start.4
  13.5 0.1 shard_map.86
  13.6 1.5 %collective-permute-start.7 = (bf16[2,272,128]{2,1,0:T(8,128)(2,1)S(1)}, bf16[2,272,128]{2,1,0:T(8,128)(2,1)S(1)}, u32[]{:S(2)}, u32[]{:S(2)}) collective-permute-start(bf16[2,272,128]{2,1,0:T(8,128)(2,1)S(1)} %get-tuple-element.83), channel_id=1, source_target_pairs={{0,4},{1,5},{2,6},{3,7},{4,0},{5,1},{6,2},{7,3},{8,12},{9,13},{10,... | collective-permute-start | bytes 417800 | tf_op jit(solution)/shard_map/ppermute | solution.py:482
  15.1 1.5 %collective-permute-start.9 = (bf16[2,272,128]{2,1,0:T(8,128)(2,1)S(1)}, bf16[2,272,128]{2,1,0:T(8,128)(2,1)S(1)}, u32[]{:S(2)}, u32[]{:S(2)}) collective-permute-start(bf16[2,272,128]{2,1,0:T(8,128)(2,1)S(1)} %get-tuple-element.85), channel_id=1, source_target_pairs={{0,5},{1,4},{2,7},{3,6},{4,1},{5,0},{6,3},{7,2},{8,13},{9,12},{10,... | collective-permute-start | bytes 417800 | tf_op jit(solution)/shard_map/ppermute | solution.py:482
  16.6 1.2 %collective-permute-start.6 = (bf16[2,272,128]{2,1,0:T(8,128)(2,1)S(1)}, bf16[2,272,128]{2,1,0:T(8,128)(2,1)S(1)}, u32[]{:S(2)}, u32[]{:S(2)}) collective-permute-start(bf16[2,272,128]{2,1,0:T(8,128)(2,1)S(1)} %get-tuple-element.82), channel_id=1, source_target_pairs={{0,9},{1,8},{2,11},{3,10},{4,13},{5,12},{6,15},{7,14},{8,1},{9,0},... | collective-permute-start | bytes 417800 | tf_op jit(solution)/shard_map/ppermute | solution.py:482
  17.8 0.8 %collective-permute-start.8 = (bf16[2,272,128]{2,1,0:T(8,128)(2,1)S(1)}, bf16[2,272,128]{2,1,0:T(8,128)(2,1)S(1)}, u32[]{:S(2)}, u32[]{:S(2)}) collective-permute-start(bf16[2,272,128]{2,1,0:T(8,128)(2,1)S(1)} %get-tuple-element.84), channel_id=1, source_target_pairs={{0,8},{1,9},{2,10},{3,11},{4,12},{5,13},{6,14},{7,15},{8,0},{9,1},... | collective-permute-start | bytes 417800 | tf_op jit(solution)/shard_map/ppermute | solution.py:482
  18.6 1.5 %collective-permute-start.5 = (bf16[2,272,128]{2,1,0:T(8,128)(2,1)S(1)}, bf16[2,272,128]{2,1,0:T(8,128)(2,1)S(1)}, u32[]{:S(2)}, u32[]{:S(2)}) collective-permute-start(bf16[2,272,128]{2,1,0:T(8,128)(2,1)S(1)} %get-tuple-element.81), channel_id=1, source_target_pairs={{0,1},{1,0},{2,3},{3,2},{4,5},{5,4},{6,7},{7,6},{8,9},{9,8},{10,11... | collective-permute-start | bytes 417800 | tf_op jit(solution)/shard_map/ppermute | solution.py:482
  20.1 0.0 collective-permute-done.7.refs_0_.refs_4_
  20.1 2.7 %collective-permute-start.3 = (bf16[2,272,128]{2,1,0:T(8,128)(2,1)S(1)}, bf16[2,272,128]{2,1,0:T(8,128)(2,1)S(1)}, u32[]{:S(2)}, u32[]{:S(2)}) collective-permute-start(bf16[2,272,128]{2,1,0:T(8,128)(2,1)S(1)} %get-tuple-element.79), channel_id=1, source_target_pairs={{0,13},{1,12},{2,15},{3,14},{4,9},{5,8},{6,11},{7,10},{8,5},{9,4},... | collective-permute-start | bytes 417800 | tf_op jit(solution)/shard_map/ppermute | solution.py:482
  22.8 0.0 collective-permute-done.9.refs_1_.refs_6_
  22.8 2.4 %collective-permute-start.4 = (bf16[2,272,128]{2,1,0:T(8,128)(2,1)S(1)}, bf16[2,272,128]{2,1,0:T(8,128)(2,1)S(1)}, u32[]{:S(2)}, u32[]{:S(2)}) collective-permute-start(bf16[2,272,128]{2,1,0:T(8,128)(2,1)S(1)} %get-tuple-element.80), channel_id=1, source_target_pairs={{0,12},{1,13},{2,14},{3,15},{4,8},{5,9},{6,10},{7,11},{8,4},{9,5},... | collective-permute-start | bytes 417800 | tf_op jit(solution)/shard_map/ppermute | solution.py:482
  25.2 0.0 copy-done.4
  25.2 0.9 %shard_map.88 = (bf16[4,128,128]{2,1,0:T(8,128)(2,1)S(1)}, bf16[4,128,128]{2,1,0:T(8,128)(2,1)S(1)}, bf16[4,128,128]{2,1,0:T(8,128)(2,1)S(1)}, bf16[4,128,128]{2...) custom-call(s32[32,128]{1,0:T(8,128)S(1)} %bitcast.1, ...), custom_call_target="tpu_custom_call" | custom-call | flops 268435456 | bytes 1343488 | tf_op jit(solution)/shard_map/pallas_call | solution.py:463
  26.2 0.0 collective-permute-done.6.refs_0_.refs_3_
  26.2 0.0 collective-permute-done.8.refs_1_.refs_5_
  26.2 0.9 %shard_map.89 = (bf16[4,128,128]{2,1,0:T(8,128)(2,1)S(1)}, bf16[4,128,128]{2,1,0:T(8,128)(2,1)S(1)}, bf16[4,128,128]{2,1,0:T(8,128)(2,1)S(1)}, bf16[4,128,128]{2...) custom-call(s32[32,128]{1,0:T(8,128)S(1)} %bitcast.2, ...), custom_call_target="tpu_custom_call" | custom-call | flops 268435456 | bytes 1343488 | tf_op jit(solution)/shard_map/pallas_call | solution.py:463
  27.1 0.6 collective-permute-done.5.refs_0_.refs_2_
  27.7 0.9 %shard_map.87 = (bf16[4,128,128]{2,1,0:T(8,128)(2,1)S(1)}, bf16[4,128,128]{2,1,0:T(8,128)(2,1)S(1)}, bf16[4,128,128]{2,1,0:T(8,128)(2,1)S(1)}, bf16[4,128,128]{2...) custom-call(s32[32,128]{1,0:T(8,128)S(1)} %bitcast.3, ...), custom_call_target="tpu_custom_call" | custom-call | flops 268435456 | bytes 1343488 | tf_op jit(solution)/shard_map/pallas_call | solution.py:463
  28.6 1.1 %collective-permute-done.3.refs_0_ = bf16[2,272,128]{2,1,0:T(8,128)(2,1)S(1)} collective-permute-done((bf16[2,272,128]{2,1,0:T(8,128)(2,1)S(1)}, bf16[2,272,128]{2,1,0:T(8,128)(2,1)S(1)}, u32[]{:S(2)}, u32[]{:S(2)}) %collective-permute-start.3) | collective-permute-done | bytes 139296 | tf_op jit(solution)/shard_map/ppermute | solution.py:482
  29.8 0.5 collective-permute-done.4.refs_1_
  30.3 0.9 %shard_map.90 = (bf16[4,128,128]{2,1,0:T(8,128)(2,1)S(1)}, bf16[4,128,128]{2,1,0:T(8,128)(2,1)S(1)}, bf16[4,128,128]{2,1,0:T(8,128)(2,1)S(1)}, bf16[4,128,128]{2...) custom-call(s32[32,128]{1,0:T(8,128)S(1)} %bitcast.4, ...), custom_call_target="tpu_custom_call" | custom-call | flops 268435456 | bytes 1343488 | tf_op jit(solution)/shard_map/pallas_call | solution.py:463
  31.3 2.2 %shard_map.91 = (bf16[4,128,128]{2,1,0:T(8,128)(2,1)S(1)}, bf16[4,128,128]{2,1,0:T(8,128)(2,1)S(1)}, bf16[4,128,128]{2,1,0:T(8,128)(2,1)S(1)}, bf16[4,128,128]{2...) custom-call(s32[32,128]{1,0:T(8,128)S(1)} %bitcast.5, ...), custom_call_target="tpu_custom_call" | custom-call | flops 268435456 | bytes 7749632 | tf_op jit(solution)/shard_map/pallas_call | solution.py:463
  33.5 1.1 %shard_map.95 = (bf16[2,272,128]{2,1,0:T(8,128)(2,1)S(1)}, bf16[2,272,128]{2,1,0:T(8,128)(2,1)S(1)}) custom-call(bf16[4,128,128]{2,1,0:T(8,128)(2,1)S(1)} %get-tuple-element.133.qb, bf16[4,128,128]{2,1,0:T(8,128)(2,1)S(1)} %get-tuple-element.92.refs_13_.ka, bf16[4,128,128]{2,1,0:T(8,128)(2,1)S(1)} %get-tuple-element.96.refs_17_.va, ...), custom_call_target="tpu_custom_call" | custom-call | flops 268435456 | bytes 1146880 | tf_op jit(solution)/shard_map/pallas_call | solution.py:463
  34.6 1.4 %collective-permute-start.14 = (bf16[2,272,128]{2,1,0:T(8,128)(2,1)S(1)}, bf16[2,272,128]{2,1,0:T(8,128)(2,1)S(1)}, u32[]{:S(2)}, u32[]{:S(2)}) collective-permute-start(bf16[2,272,128]{2,1,0:T(8,128)(2,1)S(1)} %get-tuple-element.139), channel_id=1, source_target_pairs={{0,4},{1,5},{2,6},{3,7},{4,0},{5,1},{6,2},{7,3},{8,12},{9,13},{10,... | collective-permute-start | bytes 417800 | tf_op jit(solution)/shard_map/ppermute | solution.py:482
  36.0 1.7 %collective-permute-start.16 = (bf16[2,272,128]{2,1,0:T(8,128)(2,1)S(1)}, bf16[2,272,128]{2,1,0:T(8,128)(2,1)S(1)}, u32[]{:S(2)}, u32[]{:S(2)}) collective-permute-start(bf16[2,272,128]{2,1,0:T(8,128)(2,1)S(1)} %get-tuple-element.141), channel_id=1, source_target_pairs={{0,5},{1,4},{2,7},{3,6},{4,1},{5,0},{6,3},{7,2},{8,13},{9,12},{10,... | collective-permute-start | bytes 417800 | tf_op jit(solution)/shard_map/ppermute | solution.py:482
  37.6 1.1 %shard_map.94 = (bf16[2,272,128]{2,1,0:T(8,128)(2,1)S(1)}, bf16[2,272,128]{2,1,0:T(8,128)(2,1)S(1)}) custom-call(bf16[4,128,128]{2,1,0:T(8,128)(2,1)S(1)} %get-tuple-element.126.qb, bf16[4,128,128]{2,1,0:T(8,128)(2,1)S(1)} %get-tuple-element.93.refs_14_.ka, bf16[4,128,128]{2,1,0:T(8,128)(2,1)S(1)} %get-tuple-element.97.refs_18_.va, ...), custom_call_target="tpu_custom_call" | custom-call | flops 268435456 | bytes 1146880 | tf_op jit(solution)/shard_map/pallas_call | solution.py:463
  38.7 1.6 %collective-permute-start.13 = (bf16[2,272,128]{2,1,0:T(8,128)(2,1)S(1)}, bf16[2,272,128]{2,1,0:T(8,128)(2,1)S(1)}, u32[]{:S(2)}, u32[]{:S(2)}) collective-permute-start(bf16[2,272,128]{2,1,0:T(8,128)(2,1)S(1)} %get-tuple-element.132), channel_id=1, source_target_pairs={{0,9},{1,8},{2,11},{3,10},{4,13},{5,12},{6,15},{7,14},{8,1},{9,0},... | collective-permute-start | bytes 417800 | tf_op jit(solution)/shard_map/ppermute | solution.py:482
  40.3 0.4 collective-permute-start.15
  40.8 1.1 %shard_map.93 = (bf16[2,272,128]{2,1,0:T(8,128)(2,1)S(1)}, bf16[2,272,128]{2,1,0:T(8,128)(2,1)S(1)}) custom-call(bf16[4,128,128]{2,1,0:T(8,128)(2,1)S(1)} %get-tuple-element.119.qb, bf16[4,128,128]{2,1,0:T(8,128)(2,1)S(1)} %get-tuple-element.91.refs_12_.ka, bf16[4,128,128]{2,1,0:T(8,128)(2,1)S(1)} %get-tuple-element.95.refs_16_.va, ...), custom_call_target="tpu_custom_call" | custom-call | flops 268435456 | bytes 1146880 | tf_op jit(solution)/shard_map/pallas_call | solution.py:463
  41.9 1.6 %collective-permute-start.12 = (bf16[2,272,128]{2,1,0:T(8,128)(2,1)S(1)}, bf16[2,272,128]{2,1,0:T(8,128)(2,1)S(1)}, u32[]{:S(2)}, u32[]{:S(2)}) collective-permute-start(bf16[2,272,128]{2,1,0:T(8,128)(2,1)S(1)} %get-tuple-element.125), channel_id=1, source_target_pairs={{0,1},{1,0},{2,3},{3,2},{4,5},{5,4},{6,7},{7,6},{8,9},{9,8},{10,11... | collective-permute-start | bytes 417800 | tf_op jit(solution)/shard_map/ppermute | solution.py:482
  43.4 1.1 %shard_map.92 = (bf16[2,272,128]{2,1,0:T(8,128)(2,1)S(1)}, bf16[2,272,128]{2,1,0:T(8,128)(2,1)S(1)}) custom-call(bf16[4,128,128]{2,1,0:T(8,128)(2,1)S(1)} %get-tuple-element.111.qb, bf16[4,128,128]{2,1,0:T(8,128)(2,1)S(1)} %get-tuple-element.94.refs_15_.ka, bf16[4,128,128]{2,1,0:T(8,128)(2,1)S(1)} %get-tuple-element.98.refs_19_.va, ...), custom_call_target="tpu_custom_call" | custom-call | flops 268435456 | bytes 1146880 | tf_op jit(solution)/shard_map/pallas_call | solution.py:463
  44.5 0.0 collective-permute-done.14.refs_4_
  44.5 2.6 %collective-permute-start.10 = (bf16[2,272,128]{2,1,0:T(8,128)(2,1)S(1)}, bf16[2,272,128]{2,1,0:T(8,128)(2,1)S(1)}, u32[]{:S(2)}, u32[]{:S(2)}) collective-permute-start(bf16[2,272,128]{2,1,0:T(8,128)(2,1)S(1)} %get-tuple-element.117), channel_id=1, source_target_pairs={{0,13},{1,12},{2,15},{3,14},{4,9},{5,8},{6,11},{7,10},{8,5},{9,4},... | collective-permute-start | bytes 417800 | tf_op jit(solution)/shard_map/ppermute | solution.py:482
  47.1 0.0 collective-permute-done.16.refs_6_
  47.1 0.9 %collective-permute-start.11 = (bf16[2,272,128]{2,1,0:T(8,128)(2,1)S(1)}, bf16[2,272,128]{2,1,0:T(8,128)(2,1)S(1)}, u32[]{:S(2)}, u32[]{:S(2)}) collective-permute-start(bf16[2,272,128]{2,1,0:T(8,128)(2,1)S(1)} %get-tuple-element.118), channel_id=1, source_target_pairs={{0,12},{1,13},{2,14},{3,15},{4,8},{5,9},{6,10},{7,11},{8,4},{9,5},... | collective-permute-start | bytes 417800 | tf_op jit(solution)/shard_map/ppermute | solution.py:482
  48.1 0.0 collective-permute-done.13.refs_3_
  48.1 0.0 collective-permute-done.15.refs_5_
  48.1 2.5 %collective-permute-done.12.refs_2_ = bf16[2,272,128]{2,1,0:T(8,128)(2,1)S(1)} collective-permute-done((bf16[2,272,128]{2,1,0:T(8,128)(2,1)S(1)}, bf16[2,272,128]{2,1,0:T(8,128)(2,1)S(1)}, u32[]{:S(2)}, u32[]{:S(2)}) %collective-permute-start.12) | collective-permute-done | bytes 139296 | tf_op jit(solution)/shard_map/ppermute | solution.py:482
  50.6 1.8 %collective-permute-done.10.refs_0_ = bf16[2,272,128]{2,1,0:T(8,128)(2,1)S(1)} collective-permute-done((bf16[2,272,128]{2,1,0:T(8,128)(2,1)S(1)}, bf16[2,272,128]{2,1,0:T(8,128)(2,1)S(1)}, u32[]{:S(2)}, u32[]{:S(2)}) %collective-permute-start.10) | collective-permute-done | bytes 139296 | tf_op jit(solution)/shard_map/ppermute | solution.py:482
  52.4 1.5 %collective-permute-done.11.refs_1_ = bf16[2,272,128]{2,1,0:T(8,128)(2,1)S(1)} collective-permute-done((bf16[2,272,128]{2,1,0:T(8,128)(2,1)S(1)}, bf16[2,272,128]{2,1,0:T(8,128)(2,1)S(1)}, u32[]{:S(2)}, u32[]{:S(2)}) %collective-permute-start.11) | collective-permute-done | bytes 139296 | tf_op jit(solution)/shard_map/ppermute | solution.py:482
  53.9 0.1 collective-permute-start.17
  54.0 2.5 %collective-permute-start.18 = (bf16[8,16,128]{2,1,0:T(8,128)(2,1)S(1)}, bf16[8,16,128]{2,1,0:T(8,128)(2,1)S(1)}, u32[]{:S(2)}, u32[]{:S(2)}) collective-permute-start(bf16[8,16,128]{2,1,0:T(8,128)(2,1)S(1)} %get-tuple-element.144), channel_id=1, source_target_pairs={{0,16},{1,17},{2,18},{3,19},{4,20},{5,21},{6,22},{7,23},{8,24},{9,... | collective-permute-start | bytes 98312 | tf_op jit(solution)/shard_map/ppermute | solution.py:482
  56.5 0.3 collective-permute-start.19
  56.8 2.1 %collective-permute-done.18.refs_9_ = bf16[8,16,128]{2,1,0:T(8,128)(2,1)S(1)} collective-permute-done((bf16[8,16,128]{2,1,0:T(8,128)(2,1)S(1)}, bf16[8,16,128]{2,1,0:T(8,128)(2,1)S(1)}, u32[]{:S(2)}, u32[]{:S(2)}) %collective-permute-start.18) | collective-permute-done | bytes 32800 | tf_op jit(solution)/shard_map/ppermute | solution.py:482
  58.9 1.8 %collective-permute-done.19.refs_10_ = bf16[8,16,128]{2,1,0:T(8,128)(2,1)S(1)} collective-permute-done((bf16[8,16,128]{2,1,0:T(8,128)(2,1)S(1)}, bf16[8,16,128]{2,1,0:T(8,128)(2,1)S(1)}, u32[]{:S(2)}, u32[]{:S(2)}) %collective-permute-start.19) | collective-permute-done | bytes 32800 | tf_op jit(solution)/shard_map/ppermute | solution.py:482
  60.7 0.0 collective-permute-done.17.refs_8_
  60.7 1.7 %shard_map.97 = (bf16[128,1024]{1,0:T(8,128)(2,1)}, bf16[128,1024]{1,0:T(8,128)(2,1)}, bf16[128,1024]{1,0:T(8,128)(2,1)}, bf16[128,1024]{1,0:T(8,128)(2,1)}) custom-call(bf16[2,272,128]{2,1,0:T(8,128)(2,1)S(1)} %collective-permute-done.10.refs_0_, bf16[2,272,128]{2,1,0:T(8,128)(2,1)S(1)} %collective-permute-done.11.refs_1_, ...), custom_call_target="tpu_custom_call" | custom-call | flops 134217728 | bytes 2752512 | tf_op jit(solution)/shard_map/pallas_call | solution.py:463
  (1 shorter events, 0.0 us)
Async XLA Ops:
  0.6 7.2 %copy-start.3 = (bf16[128,1024]{1,0:T(8,128)(2,1)S(1)}, bf16[128,1024]{1,0:T(8,128)(2,1)}, u32[]{:S(2)}) copy-start(bf16[128,1024]{1,0:T(8,128)(2,1)} %refs_3_.3) | copy-start | bytes 786436
  0.6 7.2 %copy-start.2 = (bf16[128,1024]{1,0:T(8,128)(2,1)S(1)}, bf16[128,1024]{1,0:T(8,128)(2,1)}, u32[]{:S(2)}) copy-start(bf16[128,1024]{1,0:T(8,128)(2,1)} %refs_2_.3) | copy-start | bytes 786436
  0.7 7.2 %copy-start.1 = (bf16[128,1024]{1,0:T(8,128)(2,1)S(1)}, bf16[128,1024]{1,0:T(8,128)(2,1)}, u32[]{:S(2)}) copy-start(bf16[128,1024]{1,0:T(8,128)(2,1)} %refs_1_.3) | copy-start | bytes 786436
  0.7 7.2 %copy-start = (bf16[128,1024]{1,0:T(8,128)(2,1)S(1)}, bf16[128,1024]{1,0:T(8,128)(2,1)}, u32[]{:S(2)}) copy-start(bf16[128,1024]{1,0:T(8,128)(2,1)} %refs_0_.3) | copy-start | bytes 786436
  3.6 9.9 %collective-permute-start = (bf16[8,256,128]{2,1,0:T(8,128)(2,1)}, bf16[8,256,128]{2,1,0:T(8,128)(2,1)S(1)}, u32[]{:S(2)}, u32[]{:S(2)}) collective-permute-start(bf16[8,256,128]{2,1,0:T(8,128)(2,1)} %get-tuple-element.76), channel_id=1, source_target_pairs={{0,2},{1,3},{2,0},{3,1},{4,6},{5,7},{6,4},{7,5},{8,10},{9,11},{10,... | collective-permute-start | bytes 1572872 | tf_op jit(solution)/shard_map/ppermute | solution.py:482
  4.1 5.6 %collective-permute-start.2 = (bf16[8,16,128]{2,1,0:T(8,128)(2,1)}, bf16[8,16,128]{2,1,0:T(8,128)(2,1)S(1)}, u32[]{:S(2)}, u32[]{:S(2)}) collective-permute-start(bf16[8,16,128]{2,1,0:T(8,128)(2,1)} %get-tuple-element.78), channel_id=1, source_target_pairs={{0,18},{1,19},{2,16},{3,17},{4,22},{5,23},{6,20},{7,21},{8,26},{9,... | collective-permute-start | bytes 98312 | tf_op jit(solution)/shard_map/ppermute | solution.py:482
  8.3 5.2 %collective-permute-start.1 = (bf16[8,16,128]{2,1,0:T(8,128)(2,1)S(1)}, bf16[8,16,128]{2,1,0:T(8,128)(2,1)S(1)}, u32[]{:S(2)}, u32[]{:S(2)}) collective-permute-start(bf16[8,16,128]{2,1,0:T(8,128)(2,1)S(1)} %get-tuple-element.77), channel_id=1, source_target_pairs={{0,16},{1,17},{2,18},{3,19},{4,20},{5,21},{6,22},{7,23},{8,24},{9,... | collective-permute-start | bytes 98312 | tf_op jit(solution)/shard_map/ppermute | solution.py:482
  13.5 11.7 %copy-start.4 = (s32[4096]{0:T(1024)S(1)}, s32[4096]{0:T(1024)}, u32[]{:S(2)}) copy-start(s32[4096]{0:T(1024)} %param.9) | copy-start | bytes 49156
  13.6 6.5 %collective-permute-start.7 = (bf16[2,272,128]{2,1,0:T(8,128)(2,1)S(1)}, bf16[2,272,128]{2,1,0:T(8,128)(2,1)S(1)}, u32[]{:S(2)}, u32[]{:S(2)}) collective-permute-start(bf16[2,272,128]{2,1,0:T(8,128)(2,1)S(1)} %get-tuple-element.83), channel_id=1, source_target_pairs={{0,4},{1,5},{2,6},{3,7},{4,0},{5,1},{6,2},{7,3},{8,12},{9,13},{10,... | collective-permute-start | bytes 417800 | tf_op jit(solution)/shard_map/ppermute | solution.py:482
  15.1 7.7 %collective-permute-start.9 = (bf16[2,272,128]{2,1,0:T(8,128)(2,1)S(1)}, bf16[2,272,128]{2,1,0:T(8,128)(2,1)S(1)}, u32[]{:S(2)}, u32[]{:S(2)}) collective-permute-start(bf16[2,272,128]{2,1,0:T(8,128)(2,1)S(1)} %get-tuple-element.85), channel_id=1, source_target_pairs={{0,5},{1,4},{2,7},{3,6},{4,1},{5,0},{6,3},{7,2},{8,13},{9,12},{10,... | collective-permute-start | bytes 417800 | tf_op jit(solution)/shard_map/ppermute | solution.py:482
  16.6 9.6 %collective-permute-start.6 = (bf16[2,272,128]{2,1,0:T(8,128)(2,1)S(1)}, bf16[2,272,128]{2,1,0:T(8,128)(2,1)S(1)}, u32[]{:S(2)}, u32[]{:S(2)}) collective-permute-start(bf16[2,272,128]{2,1,0:T(8,128)(2,1)S(1)} %get-tuple-element.82), channel_id=1, source_target_pairs={{0,9},{1,8},{2,11},{3,10},{4,13},{5,12},{6,15},{7,14},{8,1},{9,0},... | collective-permute-start | bytes 417800 | tf_op jit(solution)/shard_map/ppermute | solution.py:482
  17.8 8.4 %collective-permute-start.8 = (bf16[2,272,128]{2,1,0:T(8,128)(2,1)S(1)}, bf16[2,272,128]{2,1,0:T(8,128)(2,1)S(1)}, u32[]{:S(2)}, u32[]{:S(2)}) collective-permute-start(bf16[2,272,128]{2,1,0:T(8,128)(2,1)S(1)} %get-tuple-element.84), channel_id=1, source_target_pairs={{0,8},{1,9},{2,10},{3,11},{4,12},{5,13},{6,14},{7,15},{8,0},{9,1},... | collective-permute-start | bytes 417800 | tf_op jit(solution)/shard_map/ppermute | solution.py:482
  18.6 9.1 %collective-permute-start.5 = (bf16[2,272,128]{2,1,0:T(8,128)(2,1)S(1)}, bf16[2,272,128]{2,1,0:T(8,128)(2,1)S(1)}, u32[]{:S(2)}, u32[]{:S(2)}) collective-permute-start(bf16[2,272,128]{2,1,0:T(8,128)(2,1)S(1)} %get-tuple-element.81), channel_id=1, source_target_pairs={{0,1},{1,0},{2,3},{3,2},{4,5},{5,4},{6,7},{7,6},{8,9},{9,8},{10,11... | collective-permute-start | bytes 417800 | tf_op jit(solution)/shard_map/ppermute | solution.py:482
  20.1 9.7 %collective-permute-start.3 = (bf16[2,272,128]{2,1,0:T(8,128)(2,1)S(1)}, bf16[2,272,128]{2,1,0:T(8,128)(2,1)S(1)}, u32[]{:S(2)}, u32[]{:S(2)}) collective-permute-start(bf16[2,272,128]{2,1,0:T(8,128)(2,1)S(1)} %get-tuple-element.79), channel_id=1, source_target_pairs={{0,13},{1,12},{2,15},{3,14},{4,9},{5,8},{6,11},{7,10},{8,5},{9,4},... | collective-permute-start | bytes 417800 | tf_op jit(solution)/shard_map/ppermute | solution.py:482
  22.8 7.5 %collective-permute-start.4 = (bf16[2,272,128]{2,1,0:T(8,128)(2,1)S(1)}, bf16[2,272,128]{2,1,0:T(8,128)(2,1)S(1)}, u32[]{:S(2)}, u32[]{:S(2)}) collective-permute-start(bf16[2,272,128]{2,1,0:T(8,128)(2,1)S(1)} %get-tuple-element.80), channel_id=1, source_target_pairs={{0,12},{1,13},{2,14},{3,15},{4,8},{5,9},{6,10},{7,11},{8,4},{9,5},... | collective-permute-start | bytes 417800 | tf_op jit(solution)/shard_map/ppermute | solution.py:482
  34.6 10.0 %collective-permute-start.14 = (bf16[2,272,128]{2,1,0:T(8,128)(2,1)S(1)}, bf16[2,272,128]{2,1,0:T(8,128)(2,1)S(1)}, u32[]{:S(2)}, u32[]{:S(2)}) collective-permute-start(bf16[2,272,128]{2,1,0:T(8,128)(2,1)S(1)} %get-tuple-element.139), channel_id=1, source_target_pairs={{0,4},{1,5},{2,6},{3,7},{4,0},{5,1},{6,2},{7,3},{8,12},{9,13},{10,... | collective-permute-start | bytes 417800 | tf_op jit(solution)/shard_map/ppermute | solution.py:482
  36.0 11.2 %collective-permute-start.16 = (bf16[2,272,128]{2,1,0:T(8,128)(2,1)S(1)}, bf16[2,272,128]{2,1,0:T(8,128)(2,1)S(1)}, u32[]{:S(2)}, u32[]{:S(2)}) collective-permute-start(bf16[2,272,128]{2,1,0:T(8,128)(2,1)S(1)} %get-tuple-element.141), channel_id=1, source_target_pairs={{0,5},{1,4},{2,7},{3,6},{4,1},{5,0},{6,3},{7,2},{8,13},{9,12},{10,... | collective-permute-start | bytes 417800 | tf_op jit(solution)/shard_map/ppermute | solution.py:482
  38.7 9.4 %collective-permute-start.13 = (bf16[2,272,128]{2,1,0:T(8,128)(2,1)S(1)}, bf16[2,272,128]{2,1,0:T(8,128)(2,1)S(1)}, u32[]{:S(2)}, u32[]{:S(2)}) collective-permute-start(bf16[2,272,128]{2,1,0:T(8,128)(2,1)S(1)} %get-tuple-element.132), channel_id=1, source_target_pairs={{0,9},{1,8},{2,11},{3,10},{4,13},{5,12},{6,15},{7,14},{8,1},{9,0},... | collective-permute-start | bytes 417800 | tf_op jit(solution)/shard_map/ppermute | solution.py:482
  40.3 7.8 %collective-permute-start.15 = (bf16[2,272,128]{2,1,0:T(8,128)(2,1)S(1)}, bf16[2,272,128]{2,1,0:T(8,128)(2,1)S(1)}, u32[]{:S(2)}, u32[]{:S(2)}) collective-permute-start(bf16[2,272,128]{2,1,0:T(8,128)(2,1)S(1)} %get-tuple-element.140), channel_id=1, source_target_pairs={{0,8},{1,9},{2,10},{3,11},{4,12},{5,13},{6,14},{7,15},{8,0},{9,1},... | collective-permute-start | bytes 417800 | tf_op jit(solution)/shard_map/ppermute | solution.py:482
  41.9 8.7 %collective-permute-start.12 = (bf16[2,272,128]{2,1,0:T(8,128)(2,1)S(1)}, bf16[2,272,128]{2,1,0:T(8,128)(2,1)S(1)}, u32[]{:S(2)}, u32[]{:S(2)}) collective-permute-start(bf16[2,272,128]{2,1,0:T(8,128)(2,1)S(1)} %get-tuple-element.125), channel_id=1, source_target_pairs={{0,1},{1,0},{2,3},{3,2},{4,5},{5,4},{6,7},{7,6},{8,9},{9,8},{10,11... | collective-permute-start | bytes 417800 | tf_op jit(solution)/shard_map/ppermute | solution.py:482
  44.5 7.9 %collective-permute-start.10 = (bf16[2,272,128]{2,1,0:T(8,128)(2,1)S(1)}, bf16[2,272,128]{2,1,0:T(8,128)(2,1)S(1)}, u32[]{:S(2)}, u32[]{:S(2)}) collective-permute-start(bf16[2,272,128]{2,1,0:T(8,128)(2,1)S(1)} %get-tuple-element.117), channel_id=1, source_target_pairs={{0,13},{1,12},{2,15},{3,14},{4,9},{5,8},{6,11},{7,10},{8,5},{9,4},... | collective-permute-start | bytes 417800 | tf_op jit(solution)/shard_map/ppermute | solution.py:482
  47.1 6.8 %collective-permute-start.11 = (bf16[2,272,128]{2,1,0:T(8,128)(2,1)S(1)}, bf16[2,272,128]{2,1,0:T(8,128)(2,1)S(1)}, u32[]{:S(2)}, u32[]{:S(2)}) collective-permute-start(bf16[2,272,128]{2,1,0:T(8,128)(2,1)S(1)} %get-tuple-element.118), channel_id=1, source_target_pairs={{0,12},{1,13},{2,14},{3,15},{4,8},{5,9},{6,10},{7,11},{8,4},{9,5},... | collective-permute-start | bytes 417800 | tf_op jit(solution)/shard_map/ppermute | solution.py:482
  53.9 6.8 %collective-permute-start.17 = (bf16[8,256,128]{2,1,0:T(8,128)(2,1)S(1)}, bf16[8,256,128]{2,1,0:T(8,128)(2,1)S(1)}, u32[]{:S(2)}, u32[]{:S(2)}) collective-permute-start(bf16[8,256,128]{2,1,0:T(8,128)(2,1)S(1)} %get-tuple-element.143), channel_id=1, source_target_pairs={{0,2},{1,3},{2,0},{3,1},{4,6},{5,7},{6,4},{7,5},{8,10},{9,11},{10,... | collective-permute-start | bytes 1572872 | tf_op jit(solution)/shard_map/ppermute | solution.py:482
  54.0 4.9 %collective-permute-start.18 = (bf16[8,16,128]{2,1,0:T(8,128)(2,1)S(1)}, bf16[8,16,128]{2,1,0:T(8,128)(2,1)S(1)}, u32[]{:S(2)}, u32[]{:S(2)}) collective-permute-start(bf16[8,16,128]{2,1,0:T(8,128)(2,1)S(1)} %get-tuple-element.144), channel_id=1, source_target_pairs={{0,16},{1,17},{2,18},{3,19},{4,20},{5,21},{6,22},{7,23},{8,24},{9,... | collective-permute-start | bytes 98312 | tf_op jit(solution)/shard_map/ppermute | solution.py:482
  56.5 4.2 %collective-permute-start.19 = (bf16[8,16,128]{2,1,0:T(8,128)(2,1)S(1)}, bf16[8,16,128]{2,1,0:T(8,128)(2,1)S(1)}, u32[]{:S(2)}, u32[]{:S(2)}) collective-permute-start(bf16[8,16,128]{2,1,0:T(8,128)(2,1)S(1)} %get-tuple-element.145), channel_id=1, source_target_pairs={{0,18},{1,19},{2,16},{3,17},{4,22},{5,23},{6,20},{7,21},{8,26},{9,... | collective-permute-start | bytes 98312 | tf_op jit(solution)/shard_map/ppermute | solution.py:482

commit v2 on v0

--- a/solution.py
+++ b/solution.py
@@ -14,7 +14,7 @@
 DOC_LANE, TOTAL_LANE, QUERY_PAD, KEY_PAD = HEAD_DIM, HEAD_DIM + 3, HEAD_DIM + 6, HEAD_DIM + 7
 QUERY_TILE = 256
 FAR_ROWS = 8
-COPY_PARTS = 2
+COPY_PARTS = 4
 PACK_LIMIT = 56 * 1024 * 1024
 VMEM_LIMIT = 14 * 1024 * 1024
 
@@ -269,13 +269,6 @@
     return first, second, x - first - second
 
 
-def in_lanes(x, at):
-    first, second, third = pieces(x)
-    lane = lane_of(x.shape)
-    value = jnp.where(lane == at, first, jnp.where(lane == at + 1, second, jnp.where(lane == at + 2, third, 0.0)))
-    return value.astype(jnp.bfloat16)
-
-
 def far_kernel(plan, doc_ref, qa, ka, va, ga, acc_in, top_in, *refs):
     levels = len(plan.far)
     far_in, refs = refs[:levels], refs[levels:]
@@ -292,17 +285,34 @@
         set_rows(top, every, held, peak)
         set_rows(acc, every, held, summed)
 
-    low = lane_of((rows, LANES)) < HEAD_DIM
+    lane = lane_of((rows, LANES))
+    total, peak, dots = jnp.ones((rows, LANES), jnp.float32), *[jnp.zeros((rows, LANES), jnp.float32)] * 2
+    sums = []
     for j in every:
-        summed = jnp.concatenate([acc[j], acc_in[j, reach:]], axis=0)
-        peak = jnp.concatenate([top[j], top_in[j, reach:]], axis=0)
-        total = jnp.where(low, summed, pltpu.roll(summed, HEAD_DIM, 1))
-        normal = summed / total
-        upstream = ga[j]
-        delta = jnp.sum(normal * upstream.astype(jnp.float32), axis=1, keepdims=True)
-        qb[j] = qa[j] + in_lanes(-(peak + jnp.log(total)), TOTAL_LANE)
-        gb[j] = upstream + in_lanes(jnp.broadcast_to(-delta, (rows, LANES)), 0)
-        output[j] = normal
+        sums.append(jnp.concatenate([acc[j], acc_in[j, reach:]], axis=0))
+        dot_j = jnp.sum(sums[j] * ga[j].astype(jnp.float32), axis=1, keepdims=True)
+        total = jnp.where(lane == j, sums[j], total)
+        peak = jnp.where(lane == j, jnp.concatenate([top[j], top_in[j, reach:]], axis=0), peak)
+        dots = jnp.where(lane == j, dot_j, dots)
+    inverse = 1.0 / total
+    held_pieces = [*pieces(-(peak + jnp.log(total))), *pieces(-(dots * inverse))]
+    moved = held_pieces[0]
+    for i, piece in enumerate(held_pieces[1:]):
+        moved = moved + pltpu.roll(piece, (i + 1) * heads, 1)
+    moved = moved.astype(jnp.bfloat16)
+    column = lane_of((LANES, 2 * LANES))
+    source = lax.broadcasted_iota(jnp.int32, column.shape, 0)
+    wanted = jnp.full(column.shape, -LANES, jnp.int32)
+    for i in range(3):
+        wanted = jnp.where(column == TOTAL_LANE + i, i * heads, wanted)
+        wanted = jnp.where(column == LANES + i, (3 + i) * heads, wanted)
+    wanted = source - wanted
+    for j in every:
+        place_j = jnp.where(wanted == j, 1.0, 0.0).astype(jnp.bfloat16)
+        added = dot(moved, place_j, (1, 0)).astype(jnp.bfloat16)
+        qb[j] = qa[j] + added[:, :LANES]
+        gb[j] = ga[j] + added[:, LANES:]
+        output[j] = sums[j] * inverse[:, j : j + 1]
 
     for level, (_, held, chunks) in enumerate(plan.far):
         queries, keys, values = far_operands(plan, level, doc_ref, qb, ka, va, far_in[level])

time: 60.2 us -> 60.1 us (level)
  no operation moved by 1% of the time
where the time goes in v2:
time: 60.1 us; the launch traced here: 59.8 us
  blocking collectives  41.2 us (69%)
  Pallas kernels  12.1 us (20%)
  starting transfers between devices  4.96 us (8%)
  waiting for transfers between devices  0.85 us (1%)
  between operations  0.68 us (1%)
    all_to_all x2, blocking collectives, exchange(): return lax.all_to_all(x, axes, 0, 0, axis_index_groups=groups, tiled=True)  41.2 us
    pallas_call x6, Pallas kernels, call(): pl.pallas_call(kernel, out_shape=out_shapes, in_specs=[pl.BlockSpec(memor...  12.1 us
    ppermute x2, starting transfers between devices, from_chunk(): return lax.ppermute(x, axes, [(d, d ^ i * heads) for d in range(devices)])  4.96 us
  transfers between devices with their start and end apart: 2, of which 1 were waited for; matrix products, arithmetic and copies ran while one was open for 0% of the time, Pallas kernels for 9%

profile of v2, /device:TPU:0, one launch (start us, length us, event | category | flops | bytes accessed | tf_op | source)
XLA Modules:
  0.0 59.8 jit_solution(4875542871299089763)
XLA Ops:
  0.6 3.1 %shard_map.84 = bf16[16,2,128,128]{3,2,1,0:T(8,128)(2,1)} custom-call(bf16[128,1024]{1,0:T(8,128)(2,1)} %q_hbm.1, bf16[128,1024]{1,0:T(8,128)(2,1)} %k_hbm.1, bf16[128,1024]{1,0:T(8,128)(2,1)} %v_hbm.1, bf16[128,1024]{1,0:T(8,128)(2,1)} %g_hbm.1), custom_call_target="tpu_custom_call" | custom-call | flops 134217728 | bytes 2097152 | tf_op jit(solution)/shard_map/pallas_call | solution.py:372
  3.7 22.1 %all_to_all.10.x_ref = bf16[16,2,128,128]{3,2,1,0:T(8,128)(2,1)S(1)} all-to-all(bf16[16,2,128,128]{3,2,1,0:T(8,128)(2,1)} %shard_map.84), channel_id=1, replica_groups={{0,1,2,3,4,5,6,7,8,9,10,11,12,13,14,15},{16,17,18,19,20,21,22,23,24,25,..., dimensions={0} | all-to-all | bytes 2097152 | tf_op jit(solution)/shard_map/all_to_all | solution.py:392
  25.8 0.0 copy-start
  25.9 2.7 %collective-permute-start = (bf16[128,128]{1,0:T(8,128)(2,1)S(1)}, bf16[128,128]{1,0:T(8,128)(2,1)S(1)}, u32[]{:S(2)}, u32[]{:S(2)}) collective-permute-start(bf16[128,128]{1,0:T(8,128)(2,1)S(1)} %slice_bitcast_fusion), channel_id=1, source_target_pairs={{0,16},{1,17},{2,18},{3,19},{4,20},{5,21},{6,22},{7,23},{8,24},{9,... | collective-permute-start | bytes 98312 | tf_op jit(solution)/shard_map/ppermute | solution.py:395
  28.5 0.0 copy-done
  28.5 1.7 %shard_map.85 = (bf16[16,128,128]{2,1,0:T(8,128)(2,1)S(1)}, bf16[16,128,128]{2,1,0:T(8,128)(2,1)S(1)}, bf16[16,128,128]{2,1,0:T(8,128)(2,1)S(1)}, bf16[16,128,12...) custom-call(s32[32,128]{1,0:T(8,128)S(1)} %bitcast.8, ...), custom_call_target="tpu_custom_call" | custom-call | flops 1073741824 | bytes 5259264 | tf_op jit(solution)/shard_map/pallas_call | solution.py:372
  30.2 0.8 %collective-permute-done = bf16[128,128]{1,0:T(8,128)(2,1)S(1)} collective-permute-done((bf16[128,128]{1,0:T(8,128)(2,1)S(1)}, bf16[128,128]{1,0:T(8,128)(2,1)S(1)}, u32[]{:S(2)}, u32[]{:S(2)}) %collective-permute-start) | collective-permute-done | bytes 32800 | tf_op jit(solution)/shard_map/ppermute | solution.py:395
  31.1 1.5 %shard_map.86 = (bf16[16,128,128]{2,1,0:T(8,128)(2,1)S(1)}, bf16[16,128,128]{2,1,0:T(8,128)(2,1)S(1)}, f32[16,128,128]{2,1,0:T(8,128)S(1)}, f32[128,128]{1,0:T(8...) custom-call(s32[32,128]{1,0:T(8,128)S(1)} %bitcast.9, ...), custom_call_target="tpu_custom_call" | custom-call | flops 268435456 | bytes 6504448 | tf_op jit(solution)/shard_map/pallas_call | solution.py:372
  32.6 2.3 %collective-permute-start.1 = (bf16[128,128]{1,0:T(8,128)(2,1)S(1)}, bf16[128,128]{1,0:T(8,128)(2,1)S(1)}, u32[]{:S(2)}, u32[]{:S(2)}) collective-permute-start(bf16[128,128]{1,0:T(8,128)(2,1)S(1)} %bitcast.10), channel_id=1, source_target_pairs={{0,16},{1,17},{2,18},{3,19},{4,20},{5,21},{6,22},{7,23},{8,24},{9,... | collective-permute-start | bytes 98312 | tf_op jit(solution)/shard_map/ppermute | solution.py:395
  34.9 3.7 %shard_map.87 = (f32[16,128,128]{2,1,0:T(8,128)S(1)}, f32[16,128,128]{2,1,0:T(8,128)S(1)}) custom-call(bf16[16,128,128]{2,1,0:T(8,128)(2,1)S(1)} %get-tuple-element.24.qb, bf16[16,128,128]{2,1,0:T(8,128)(2,1)S(1)} %get-tuple-element.19.ka, bf16[16,128,128]{2,1,0:T(8,128)(2,1)S(1)} %get-tuple-element.20.va, bf16[16,128,128]{2,1,0:T(8,128)(2,1)S(1)} %get-tuple-element.25.gb), custom_call_target="tpu_custom_call" | custom-call | flops 1073741824 | bytes 4194304 | tf_op jit(solution)/shard_map/pallas_call | solution.py:372
  38.7 0.0 collective-permute-done.1
  38.7 0.6 shard_map.88
  39.3 19.1 %all_to_all.11.in_ref = bf16[16,2,128,128]{3,2,1,0:T(8,128)(2,1)S(1)} all-to-all(bf16[16,2,128,128]{3,2,1,0:T(8,128)(2,1)S(1)} %shard_map.88), channel_id=1, replica_groups={{0,1,2,3,4,5,6,7,8,9,10,11,12,13,14,15},{16,17,18,19,20,21,22,23,24,25,..., dimensions={0} | all-to-all | bytes 2097152 | tf_op jit(solution)/shard_map/all_to_all | solution.py:392
  58.3 1.4 %shard_map.89 = (bf16[128,1024]{1,0:T(8,128)(2,1)}, bf16[128,1024]{1,0:T(8,128)(2,1)}, bf16[128,1024]{1,0:T(8,128)(2,1)}, bf16[128,1024]{1,0:T(8,128)(2,1)}) custom-call(bf16[16,2,128,128]{3,2,1,0:T(8,128)(2,1)S(1)} %all_to_all.11.in_ref), custom_call_target="tpu_custom_call" | custom-call | flops 134217728 | bytes 2097152 | tf_op jit(solution)/shard_map/pallas_call | solution.py:372
  (1 shorter events, 0.0 us)
Async XLA Ops:
  25.8 2.7 %copy-start = (s32[4096]{0:T(1024)S(1)}, s32[4096]{0:T(1024)}, u32[]{:S(2)}) copy-start(s32[4096]{0:T(1024)} %param.9) | copy-start | bytes 49156
  25.9 5.2 %collective-permute-start = (bf16[128,128]{1,0:T(8,128)(2,1)S(1)}, bf16[128,128]{1,0:T(8,128)(2,1)S(1)}, u32[]{:S(2)}, u32[]{:S(2)}) collective-permute-start(bf16[128,128]{1,0:T(8,128)(2,1)S(1)} %slice_bitcast_fusion), channel_id=1, source_target_pairs={{0,16},{1,17},{2,18},{3,19},{4,20},{5,21},{6,22},{7,23},{8,24},{9,... | collective-permute-start | bytes 98312 | tf_op jit(solution)/shard_map/ppermute | solution.py:395
  32.6 6.0 %collective-permute-start.1 = (bf16[128,128]{1,0:T(8,128)(2,1)S(1)}, bf16[128,128]{1,0:T(8,128)(2,1)S(1)}, u32[]{:S(2)}, u32[]{:S(2)}) collective-permute-start(bf16[128,128]{1,0:T(8,128)(2,1)S(1)} %bitcast.10), channel_id=1, source_target_pairs={{0,16},{1,17},{2,18},{3,19},{4,20},{5,21},{6,22},{7,23},{8,24},{9,... | collective-permute-start | bytes 98312 | tf_op jit(solution)/shard_map/ppermute | solution.py:395

commit v3 on v2

--- a/solution.py
+++ b/solution.py
@@ -14,7 +14,7 @@
 DOC_LANE, TOTAL_LANE, QUERY_PAD, KEY_PAD = HEAD_DIM, HEAD_DIM + 3, HEAD_DIM + 6, HEAD_DIM + 7
 QUERY_TILE = 256
 FAR_ROWS = 8
-COPY_PARTS = 4
+COPY_PARTS = 2
 PACK_LIMIT = 56 * 1024 * 1024
 VMEM_LIMIT = 14 * 1024 * 1024
 
@@ -48,37 +48,31 @@
 
 def pack_kernel(rates, q_hbm, k_hbm, v_hbm, g_hbm, out_hbm, q_ref, k_ref, v_ref, g_ref, out_ref, arrived, left):
     rows, width = q_ref.shape
-    copies, outgoing = [], []
-    for part in range(COPY_PARTS):
-        cols = pl.ds(part * (width // COPY_PARTS), width // COPY_PARTS)
-        held = ((q_hbm, q_ref), (k_hbm, k_ref), (v_hbm, v_ref), (g_hbm, g_ref))
-        copies.append(
-            [pltpu.make_async_copy(a.at[:, cols], b.at[:, cols], arrived.at[part, i]) for i, (a, b) in enumerate(held)]
-        )
-    for part in copies:
-        for copy in part:
-            copy.start()
+    heads = width // HEAD_DIM
+    held = ((k_hbm, k_ref), (v_hbm, v_ref), (q_hbm, q_ref), (g_hbm, g_ref))
+    copies = [pltpu.make_async_copy(a, b, arrived.at[i]) for i, (a, b) in enumerate(held)]
+    for copy in copies:
+        copy.start()
     order = row_order(rows, rates, (rows, rows), 0)
     lane = lane_of((rows, rows))
     low, high = lane_mask(rows, 1.0, 0.0), lane_mask(rows, 0.0, 1.0)
-    for tile in range(width // LANES):
-        cols = slice(tile * LANES, (tile + 1) * LANES)
-        part, inside = divmod(tile * LANES, width // COPY_PARTS)
-        if inside == 0:
-            for copy in copies[part]:
-                copy.wait()
-        pairs = ((q_ref[:, cols], g_ref[:, cols]), (k_ref[:, cols], v_ref[:, cols]))
-        even = [first * low + halves_swapped(second) * high for first, second in pairs]
-        odd = [halves_swapped(first) * low + second * high for first, second in pairs]
-        for side, sources in enumerate((even, odd)):
-            pick = jnp.where(order == ((lane - (2 * tile + side)) & (rows - 1)), 1.0, 0.0).astype(jnp.bfloat16)
-            moved = dot(pick, jnp.concatenate(sources, axis=1), (1, 0)).astype(jnp.bfloat16)
-            out_ref[2 * tile + side, 0] = moved[:, :LANES]
-            out_ref[2 * tile + side, 1] = moved[:, LANES:]
-        if inside + LANES == width // COPY_PARTS:
-            done = pl.ds(part * (width // HEAD_DIM // COPY_PARTS), width // HEAD_DIM // COPY_PARTS)
-            outgoing.append(pltpu.make_async_copy(out_ref.at[done], out_hbm.at[done], left.at[part]))
-            outgoing[-1].start()
+    outgoing = []
+    for kind, first_ref, second_ref, waits in ((1, k_ref, v_ref, copies[:2]), (0, q_ref, g_ref, copies[2:])):
+        for copy in waits:
+            copy.wait()
+        for tile in range(width // LANES):
+            cols = slice(tile * LANES, (tile + 1) * LANES)
+            first, second = first_ref[:, cols], second_ref[:, cols]
+            even = first * low + halves_swapped(second) * high
+            odd = halves_swapped(first) * low + second * high
+            for side, source in enumerate((even, odd)):
+                pick = jnp.where(order == ((lane - (2 * tile + side)) & (rows - 1)), 1.0, 0.0).astype(jnp.bfloat16)
+                out_ref[2 * tile + side, kind] = dot(pick, source, (1, 0)).astype(jnp.bfloat16)
+            if (2 * tile + 2) % (heads // COPY_PARTS) == 0:
+                done = pl.ds(2 * tile + 2 - heads // COPY_PARTS, heads // COPY_PARTS)
+                ready = left.at[kind, (2 * tile + 1) // (heads // COPY_PARTS)]
+                outgoing.append(pltpu.make_async_copy(out_ref.at[done, kind], out_hbm.at[done, kind], ready))
+                outgoing[-1].start()
     for copy in outgoing:
         copy.wait()
 
@@ -223,7 +217,9 @@
     for_keys = dot(shifted, queries, (1, 0))
     for_values = dot(probability.astype(jnp.bfloat16), upstream, (1, 0))
     key_low = lane_of(for_keys.shape) < HEAD_DIM
-    return dot(shifted, keys, (0, 0)), jnp.where(key_low, for_keys, for_values)
+    for_queries = dot(keys.T[:HEAD_DIM], shifted, (1, 0)).T
+    for_queries = jnp.concatenate([for_queries, jnp.zeros_like(for_queries)], axis=1)
+    return for_queries, jnp.where(key_low, for_keys, for_values)
 
 
 def merged(old_peak, old, peak, summed):
@@ -406,7 +402,8 @@
 
     inputs = (queries, keys, values, grad_out)
     semaphores = pltpu.SemaphoreType.DMA((COPY_PARTS, len(inputs)))
-    landing = [landed(x) for x in (*inputs, packed)] + [semaphores, pltpu.SemaphoreType.DMA((COPY_PARTS,))]
+    landing = [landed(x) for x in (*inputs, packed)]
+    landing += [pltpu.SemaphoreType.DMA((len(inputs),)), pltpu.SemaphoreType.DMA((2, COPY_PARTS))]
     mine = call(
         functools.partial(pack_kernel, plan.rates), [packed], inputs, landing, flops=1 << 27, inputs=pltpu.HBM, outputs=pltpu.HBM, limit=PACK_LIMIT
     )[0]

time: 60.1 us -> 58.8 us (0.978)
  Pallas kernels: 12.1 us -> 10.8 us
    pallas_call x6, Pallas kernels: 12.1 us -> 10.8 us  [call(): pl.pallas_call(kernel, out_shape=out_shapes, in_specs=[pl.BlockSpec(memor...]
  transfers between devices with their start and end apart: 2 -> 2, of which waited for: 1 -> 1; matrix products, arithmetic and copies ran while one was open for 0% -> 0% of each run, Pallas kernels for 9% -> 8%
where the time goes in v3:
time: 58.8 us; the launch traced here: 58.5 us
  blocking collectives  41.2 us (70%)
  Pallas kernels  10.8 us (18%)
  starting transfers between devices  4.95 us (8%)
  waiting for transfers between devices  0.85 us (1%)
  between operations  0.68 us (1%)
    all_to_all x2, blocking collectives, exchange(): return lax.all_to_all(x, axes, 0, 0, axis_index_groups=groups, tiled=True)  41.2 us
    pallas_call x6, Pallas kernels, call(): pl.pallas_call(kernel, out_shape=out_shapes, in_specs=[pl.BlockSpec(memor...  10.8 us
    ppermute x2, starting transfers between devices, from_chunk(): return lax.ppermute(x, axes, [(d, d ^ i * heads) for d in range(devices)])  4.95 us
  transfers between devices with their start and end apart: 2, of which 1 were waited for; matrix products, arithmetic and copies ran while one was open for 0% of the time, Pallas kernels for 8%

profile of v3, /device:TPU:0, one launch (start us, length us, event | category | flops | bytes accessed | tf_op | source)
XLA Modules:
  0.0 58.5 jit_solution(10388232898305631449)
XLA Ops:
  0.6 2.6 %shard_map.84 = bf16[16,2,128,128]{3,2,1,0:T(8,128)(2,1)} custom-call(bf16[128,1024]{1,0:T(8,128)(2,1)} %q_hbm.1, bf16[128,1024]{1,0:T(8,128)(2,1)} %k_hbm.1, bf16[128,1024]{1,0:T(8,128)(2,1)} %v_hbm.1, bf16[128,1024]{1,0:T(8,128)(2,1)} %g_hbm.1), custom_call_target="tpu_custom_call" | custom-call | flops 134217728 | bytes 2097152 | tf_op jit(solution)/shard_map/pallas_call | solution.py:368
  3.2 22.1 %all_to_all.10.x_ref = bf16[16,2,128,128]{3,2,1,0:T(8,128)(2,1)S(1)} all-to-all(bf16[16,2,128,128]{3,2,1,0:T(8,128)(2,1)} %shard_map.84), channel_id=1, replica_groups={{0,1,2,3,4,5,6,7,8,9,10,11,12,13,14,15},{16,17,18,19,20,21,22,23,24,25,..., dimensions={0} | all-to-all | bytes 2097152 | tf_op jit(solution)/shard_map/all_to_all | solution.py:388
  25.4 0.0 copy-start
  25.4 2.7 %collective-permute-start = (bf16[128,128]{1,0:T(8,128)(2,1)S(1)}, bf16[128,128]{1,0:T(8,128)(2,1)S(1)}, u32[]{:S(2)}, u32[]{:S(2)}) collective-permute-start(bf16[128,128]{1,0:T(8,128)(2,1)S(1)} %slice_bitcast_fusion), channel_id=1, source_target_pairs={{0,16},{1,17},{2,18},{3,19},{4,20},{5,21},{6,22},{7,23},{8,24},{9,... | collective-permute-start | bytes 98312 | tf_op jit(solution)/shard_map/ppermute | solution.py:391
  28.0 0.0 copy-done
  28.0 1.7 %shard_map.85 = (bf16[16,128,128]{2,1,0:T(8,128)(2,1)S(1)}, bf16[16,128,128]{2,1,0:T(8,128)(2,1)S(1)}, bf16[16,128,128]{2,1,0:T(8,128)(2,1)S(1)}, bf16[16,128,12...) custom-call(s32[32,128]{1,0:T(8,128)S(1)} %bitcast.8, ...), custom_call_target="tpu_custom_call" | custom-call | flops 1073741824 | bytes 5259264 | tf_op jit(solution)/shard_map/pallas_call | solution.py:368
  29.8 0.8 %collective-permute-done = bf16[128,128]{1,0:T(8,128)(2,1)S(1)} collective-permute-done((bf16[128,128]{1,0:T(8,128)(2,1)S(1)}, bf16[128,128]{1,0:T(8,128)(2,1)S(1)}, u32[]{:S(2)}, u32[]{:S(2)}) %collective-permute-start) | collective-permute-done | bytes 32800 | tf_op jit(solution)/shard_map/ppermute | solution.py:391
  30.6 1.5 %shard_map.86 = (bf16[16,128,128]{2,1,0:T(8,128)(2,1)S(1)}, bf16[16,128,128]{2,1,0:T(8,128)(2,1)S(1)}, f32[16,128,128]{2,1,0:T(8,128)S(1)}, f32[128,128]{1,0:T(8...) custom-call(s32[32,128]{1,0:T(8,128)S(1)} %bitcast.9, ...), custom_call_target="tpu_custom_call" | custom-call | flops 268435456 | bytes 6504448 | tf_op jit(solution)/shard_map/pallas_call | solution.py:368
  32.2 2.3 %collective-permute-start.1 = (bf16[128,128]{1,0:T(8,128)(2,1)S(1)}, bf16[128,128]{1,0:T(8,128)(2,1)S(1)}, u32[]{:S(2)}, u32[]{:S(2)}) collective-permute-start(bf16[128,128]{1,0:T(8,128)(2,1)S(1)} %bitcast.10), channel_id=1, source_target_pairs={{0,16},{1,17},{2,18},{3,19},{4,20},{5,21},{6,22},{7,23},{8,24},{9,... | collective-permute-start | bytes 98312 | tf_op jit(solution)/shard_map/ppermute | solution.py:391
  34.5 3.0 %shard_map.87 = (f32[16,128,128]{2,1,0:T(8,128)S(1)}, f32[16,128,128]{2,1,0:T(8,128)S(1)}) custom-call(bf16[16,128,128]{2,1,0:T(8,128)(2,1)S(1)} %get-tuple-element.24.qb, bf16[16,128,128]{2,1,0:T(8,128)(2,1)S(1)} %get-tuple-element.19.ka, bf16[16,128,128]{2,1,0:T(8,128)(2,1)S(1)} %get-tuple-element.20.va, bf16[16,128,128]{2,1,0:T(8,128)(2,1)S(1)} %get-tuple-element.25.gb), custom_call_target="tpu_custom_call" | custom-call | flops 1073741824 | bytes 4194304 | tf_op jit(solution)/shard_map/pallas_call | solution.py:368
  37.4 0.0 collective-permute-done.1
  37.5 0.5 shard_map.88
  38.0 19.1 %all_to_all.11.in_ref = bf16[16,2,128,128]{3,2,1,0:T(8,128)(2,1)S(1)} all-to-all(bf16[16,2,128,128]{3,2,1,0:T(8,128)(2,1)S(1)} %shard_map.88), channel_id=1, replica_groups={{0,1,2,3,4,5,6,7,8,9,10,11,12,13,14,15},{16,17,18,19,20,21,22,23,24,25,..., dimensions={0} | all-to-all | bytes 2097152 | tf_op jit(solution)/shard_map/all_to_all | solution.py:388
  57.1 1.4 %shard_map.89 = (bf16[128,1024]{1,0:T(8,128)(2,1)}, bf16[128,1024]{1,0:T(8,128)(2,1)}, bf16[128,1024]{1,0:T(8,128)(2,1)}, bf16[128,1024]{1,0:T(8,128)(2,1)}) custom-call(bf16[16,2,128,128]{3,2,1,0:T(8,128)(2,1)S(1)} %all_to_all.11.in_ref), custom_call_target="tpu_custom_call" | custom-call | flops 134217728 | bytes 2097152 | tf_op jit(solution)/shard_map/pallas_call | solution.py:368
  (1 shorter events, 0.0 us)
Async XLA Ops:
  25.4 2.7 %copy-start = (s32[4096]{0:T(1024)S(1)}, s32[4096]{0:T(1024)}, u32[]{:S(2)}) copy-start(s32[4096]{0:T(1024)} %param.9) | copy-start | bytes 49156
  25.4 5.2 %collective-permute-start = (bf16[128,128]{1,0:T(8,128)(2,1)S(1)}, bf16[128,128]{1,0:T(8,128)(2,1)S(1)}, u32[]{:S(2)}, u32[]{:S(2)}) collective-permute-start(bf16[128,128]{1,0:T(8,128)(2,1)S(1)} %slice_bitcast_fusion), channel_id=1, source_target_pairs={{0,16},{1,17},{2,18},{3,19},{4,20},{5,21},{6,22},{7,23},{8,24},{9,... | collective-permute-start | bytes 98312 | tf_op jit(solution)/shard_map/ppermute | solution.py:391
  32.2 5.3 %collective-permute-start.1 = (bf16[128,128]{1,0:T(8,128)(2,1)S(1)}, bf16[128,128]{1,0:T(8,128)(2,1)S(1)}, u32[]{:S(2)}, u32[]{:S(2)}) collective-permute-start(bf16[128,128]{1,0:T(8,128)(2,1)S(1)} %bitcast.10), channel_id=1, source_target_pairs={{0,16},{1,17},{2,18},{3,19},{4,20},{5,21},{6,22},{7,23},{8,24},{9,... | collective-permute-start | bytes 98312 | tf_op jit(solution)/shard_map/ppermute | solution.py:391

commit v4 on v3

--- a/solution.py
+++ b/solution.py
@@ -84,28 +84,23 @@
     order = row_order(rows, rates, (rows, rows), 1)
     token = lax.broadcasted_iota(jnp.int32, (rows, rows), 0)
     low, high = lane_mask(rows, 1.0, 0.0), lane_mask(rows, 0.0, 1.0)
-    for tile in range(width // LANES):
-        cols = slice(tile * LANES, (tile + 1) * LANES)
-        picks, sources = [], []
-        for side in range(2):
-            head = 2 * tile + side
-            picks.append(jnp.where(((order + head) & (rows - 1)) == token, 1.0, 0.0).astype(jnp.bfloat16))
-            columns = []
-            for kind in range(2):
+    held = ((dq_ref, dq_hbm), (out_ref, out_hbm), (dk_ref, dk_hbm), (dv_ref, dv_hbm))
+    for kind in range(2):
+        for tile in range(width // LANES):
+            cols = slice(tile * LANES, (tile + 1) * LANES)
+            picks, sources = [], []
+            for side in range(2):
+                head = 2 * tile + side
+                picks.append(jnp.where(((order + head) & (rows - 1)) == token, 1.0, 0.0).astype(jnp.bfloat16))
                 x = in_ref[head, kind]
                 y = halves_swapped(x)
-                columns += [y * high, x * high] if side else [x * low, y * low]
-            sources.append(jnp.concatenate(columns, axis=1))
-        moved = dot(jnp.concatenate(picks, axis=1), jnp.concatenate(sources, axis=0), (1, 0)).astype(jnp.bfloat16)
-        for i, ref in enumerate((dq_ref, out_ref, dk_ref, dv_ref)):
-            ref[:, cols] = moved[:, i * LANES : (i + 1) * LANES]
-        part, inside = divmod((tile + 1) * LANES, width // COPY_PARTS)
-        if inside == 0:
-            done = pl.ds((part - 1) * (width // COPY_PARTS), width // COPY_PARTS)
-            held = ((out_ref, out_hbm), (dq_ref, dq_hbm), (dk_ref, dk_hbm), (dv_ref, dv_hbm))
-            for i, (a, b) in enumerate(held):
-                outgoing.append(pltpu.make_async_copy(a.at[:, done], b.at[:, done], left.at[part - 1, i]))
-                outgoing[-1].start()
+                sources.append(jnp.concatenate([y * high, x * high] if side else [x * low, y * low], axis=1))
+            moved = dot(jnp.concatenate(picks, axis=1), jnp.concatenate(sources, axis=0), (1, 0)).astype(jnp.bfloat16)
+            for i in range(2):
+                held[2 * kind + i][0][:, cols] = moved[:, i * LANES : (i + 1) * LANES]
+        for i in range(2 * kind, 2 * kind + 2):
+            outgoing.append(pltpu.make_async_copy(*held[i], left.at[0, i]))
+            outgoing[-1].start()
     for copy in outgoing:
         copy.wait()
 

time: 58.8 us -> 58.8 us (level)
  no operation moved by 1% of the time
where the time goes in v4:
time: 58.8 us; the launch traced here: 58.5 us
  blocking collectives  41.2 us (70%)
  Pallas kernels  10.9 us (19%)
  starting transfers between devices  4.95 us (8%)
  waiting for transfers between devices  0.85 us (1%)
  between operations  0.68 us (1%)
    all_to_all x2, blocking collectives, exchange(): return lax.all_to_all(x, axes, 0, 0, axis_index_groups=groups, tiled=True)  41.2 us
    pallas_call x6, Pallas kernels, call(): pl.pallas_call(kernel, out_shape=out_shapes, in_specs=[pl.BlockSpec(memor...  10.9 us
    ppermute x2, starting transfers between devices, from_chunk(): return lax.ppermute(x, axes, [(d, d ^ i * heads) for d in range(devices)])  4.95 us
  transfers between devices with their start and end apart: 2, of which 1 were waited for; matrix products, arithmetic and copies ran while one was open for 0% of the time, Pallas kernels for 8%

profile of v4, /device:TPU:0, one launch (start us, length us, event | category | flops | bytes accessed | tf_op | source)
XLA Modules:
  0.0 58.5 jit_solution(5621569389137990080)
XLA Ops:
  0.6 2.6 %shard_map.84 = bf16[16,2,128,128]{3,2,1,0:T(8,128)(2,1)} custom-call(bf16[128,1024]{1,0:T(8,128)(2,1)} %q_hbm.1, bf16[128,1024]{1,0:T(8,128)(2,1)} %k_hbm.1, bf16[128,1024]{1,0:T(8,128)(2,1)} %v_hbm.1, bf16[128,1024]{1,0:T(8,128)(2,1)} %g_hbm.1), custom_call_target="tpu_custom_call" | custom-call | flops 134217728 | bytes 2097152 | tf_op jit(solution)/shard_map/pallas_call | solution.py:363
  3.2 22.1 %all_to_all.10.x_ref = bf16[16,2,128,128]{3,2,1,0:T(8,128)(2,1)S(1)} all-to-all(bf16[16,2,128,128]{3,2,1,0:T(8,128)(2,1)} %shard_map.84), channel_id=1, replica_groups={{0,1,2,3,4,5,6,7,8,9,10,11,12,13,14,15},{16,17,18,19,20,21,22,23,24,25,..., dimensions={0} | all-to-all | bytes 2097152 | tf_op jit(solution)/shard_map/all_to_all | solution.py:383
  25.4 0.0 copy-start
  25.4 2.7 %collective-permute-start = (bf16[128,128]{1,0:T(8,128)(2,1)S(1)}, bf16[128,128]{1,0:T(8,128)(2,1)S(1)}, u32[]{:S(2)}, u32[]{:S(2)}) collective-permute-start(bf16[128,128]{1,0:T(8,128)(2,1)S(1)} %slice_bitcast_fusion), channel_id=1, source_target_pairs={{0,16},{1,17},{2,18},{3,19},{4,20},{5,21},{6,22},{7,23},{8,24},{9,... | collective-permute-start | bytes 98312 | tf_op jit(solution)/shard_map/ppermute | solution.py:386
  28.0 0.0 copy-done
  28.0 1.7 %shard_map.85 = (bf16[16,128,128]{2,1,0:T(8,128)(2,1)S(1)}, bf16[16,128,128]{2,1,0:T(8,128)(2,1)S(1)}, bf16[16,128,128]{2,1,0:T(8,128)(2,1)S(1)}, bf16[16,128,12...) custom-call(s32[32,128]{1,0:T(8,128)S(1)} %bitcast.8, ...), custom_call_target="tpu_custom_call" | custom-call | flops 1073741824 | bytes 5259264 | tf_op jit(solution)/shard_map/pallas_call | solution.py:363
  29.8 0.8 %collective-permute-done = bf16[128,128]{1,0:T(8,128)(2,1)S(1)} collective-permute-done((bf16[128,128]{1,0:T(8,128)(2,1)S(1)}, bf16[128,128]{1,0:T(8,128)(2,1)S(1)}, u32[]{:S(2)}, u32[]{:S(2)}) %collective-permute-start) | collective-permute-done | bytes 32800 | tf_op jit(solution)/shard_map/ppermute | solution.py:386
  30.6 1.5 %shard_map.86 = (bf16[16,128,128]{2,1,0:T(8,128)(2,1)S(1)}, bf16[16,128,128]{2,1,0:T(8,128)(2,1)S(1)}, f32[16,128,128]{2,1,0:T(8,128)S(1)}, f32[128,128]{1,0:T(8...) custom-call(s32[32,128]{1,0:T(8,128)S(1)} %bitcast.9, ...), custom_call_target="tpu_custom_call" | custom-call | flops 268435456 | bytes 6504448 | tf_op jit(solution)/shard_map/pallas_call | solution.py:363
  32.2 2.3 %collective-permute-start.1 = (bf16[128,128]{1,0:T(8,128)(2,1)S(1)}, bf16[128,128]{1,0:T(8,128)(2,1)S(1)}, u32[]{:S(2)}, u32[]{:S(2)}) collective-permute-start(bf16[128,128]{1,0:T(8,128)(2,1)S(1)} %bitcast.10), channel_id=1, source_target_pairs={{0,16},{1,17},{2,18},{3,19},{4,20},{5,21},{6,22},{7,23},{8,24},{9,... | collective-permute-start | bytes 98312 | tf_op jit(solution)/shard_map/ppermute | solution.py:386
  34.5 3.0 %shard_map.87 = (f32[16,128,128]{2,1,0:T(8,128)S(1)}, f32[16,128,128]{2,1,0:T(8,128)S(1)}) custom-call(bf16[16,128,128]{2,1,0:T(8,128)(2,1)S(1)} %get-tuple-element.24.qb, bf16[16,128,128]{2,1,0:T(8,128)(2,1)S(1)} %get-tuple-element.19.ka, bf16[16,128,128]{2,1,0:T(8,128)(2,1)S(1)} %get-tuple-element.20.va, bf16[16,128,128]{2,1,0:T(8,128)(2,1)S(1)} %get-tuple-element.25.gb), custom_call_target="tpu_custom_call" | custom-call | flops 1073741824 | bytes 4194304 | tf_op jit(solution)/shard_map/pallas_call | solution.py:363
  37.4 0.0 collective-permute-done.1
  37.5 0.5 shard_map.88
  38.0 19.1 %all_to_all.11.in_ref = bf16[16,2,128,128]{3,2,1,0:T(8,128)(2,1)S(1)} all-to-all(bf16[16,2,128,128]{3,2,1,0:T(8,128)(2,1)S(1)} %shard_map.88), channel_id=1, replica_groups={{0,1,2,3,4,5,6,7,8,9,10,11,12,13,14,15},{16,17,18,19,20,21,22,23,24,25,..., dimensions={0} | all-to-all | bytes 2097152 | tf_op jit(solution)/shard_map/all_to_all | solution.py:383
  57.1 1.5 %shard_map.89 = (bf16[128,1024]{1,0:T(8,128)(2,1)}, bf16[128,1024]{1,0:T(8,128)(2,1)}, bf16[128,1024]{1,0:T(8,128)(2,1)}, bf16[128,1024]{1,0:T(8,128)(2,1)}) custom-call(bf16[16,2,128,128]{3,2,1,0:T(8,128)(2,1)S(1)} %all_to_all.11.in_ref), custom_call_target="tpu_custom_call" | custom-call | flops 134217728 | bytes 2097152 | tf_op jit(solution)/shard_map/pallas_call | solution.py:363
  (1 shorter events, 0.0 us)
Async XLA Ops:
  25.4 2.7 %copy-start = (s32[4096]{0:T(1024)S(1)}, s32[4096]{0:T(1024)}, u32[]{:S(2)}) copy-start(s32[4096]{0:T(1024)} %param.9) | copy-start | bytes 49156
  25.4 5.2 %collective-permute-start = (bf16[128,128]{1,0:T(8,128)(2,1)S(1)}, bf16[128,128]{1,0:T(8,128)(2,1)S(1)}, u32[]{:S(2)}, u32[]{:S(2)}) collective-permute-start(bf16[128,128]{1,0:T(8,128)(2,1)S(1)} %slice_bitcast_fusion), channel_id=1, source_target_pairs={{0,16},{1,17},{2,18},{3,19},{4,20},{5,21},{6,22},{7,23},{8,24},{9,... | collective-permute-start | bytes 98312 | tf_op jit(solution)/shard_map/ppermute | solution.py:386
  32.2 5.3 %collective-permute-start.1 = (bf16[128,128]{1,0:T(8,128)(2,1)S(1)}, bf16[128,128]{1,0:T(8,128)(2,1)S(1)}, u32[]{:S(2)}, u32[]{:S(2)}) collective-permute-start(bf16[128,128]{1,0:T(8,128)(2,1)S(1)} %bitcast.10), channel_id=1, source_target_pairs={{0,16},{1,17},{2,18},{3,19},{4,20},{5,21},{6,22},{7,23},{8,24},{9,... | collective-permute-start | bytes 98312 | tf_op jit(solution)/shard_map/ppermute | solution.py:386
